TPU v7x, 32 devices: a whole 2x2x4 slice. The times are simulated.
32 devices in a mesh: blk: 8 (over y, x, core), tp: 4 (over z).
Axes of the slice: x: 2, y: 2, z: 4, core: 2. Of those that a mesh axis runs over, the one named last changes fastest.
Arguments:
- hidden_in: bfloat16 [4096, 6144], P('blk', 'tp'), may hold values from -40 to 40
- ln_gain: float32 [6144], replicated, may hold values from 0.1 to 1.9
- w_qkv: bfloat16 [6144, 3, 3072], P(None, None, 'tp'), may hold values from -1 to 1
- w_out: bfloat16 [3072, 6144], P('tp'), may hold values from -0.625 to 0.625
- doc_lengths: int32 [32], replicated, may hold values from 0 to 2048, as said below
- segment_ids: int32 [4096], P('blk'), may hold values from 0 to 31, as said below
- pair_table: int32 [8, 8], replicated, may hold values from 0 to 1, as said below
- page_table: int32 [256], P('blk'), may hold values from 0 to 255, as said below
Outputs:
- attn_out: bfloat16 [4096, 6144], P('blk', 'tp')
- page_cache: bfloat16 [2, 256, 16, 3072], P(None, 'blk', None, 'tp')
Inputs may be any that keep to these rules, and one draw needn't show every extreme that they name: `doc_lengths`: the 32 documents in stream order; they sum to 4096, the empty ones stand just before the last slot, which holds the stream's last document, and the second document has exactly 2048 tokens. segment_ids[t] is the number of documents that end at or before token t; the last token belongs to slot 31. pair_table[i, j] is 1 exactly where a token of block j of 512 tokens and a token at or after it in block i lie in one document. `page_table`: the 32 entries of one block of tokens are that block's own page numbers, each once.
All inputs are finite; a program needn't handle non-finite values.
Results may differ from a plain program's by a relative error of at most 0.014.
Values may be sent and summed in bfloat16 or wider, within the bound.
No kernel may reach another device: no remote copies, remote signals or barrier semaphores. Data moves between devices by JAX's collectives and lax.ppermute only.
A program may use at most 256 MiB of HBM per device.

v0:
```python
import functools

import jax
import jax.numpy as jnp
from jax import lax
from jax.experimental import pallas as pl
from jax.experimental.pallas import tpu as pltpu
from jax.sharding import PartitionSpec as P

HD = 96
ROT = 24
PAGE = 16


EPSILON = 1e-05


def from_behind(value, axis, steps):
    count = lax.axis_size(axis)
    first, last = (max(0, -steps), min(count, count - steps))
    return lax.ppermute(value, axis, [(source, source + steps) for source in range(first, last)])


def layer_norm(whole, ln_gain):
    values32 = whole.astype(jnp.float32)
    row_mean = jnp.mean(values32, axis=-1, keepdims=True)
    centred = values32 - row_mean
    row_var = jnp.mean(centred * centred, axis=-1, keepdims=True)
    return (centred * lax.rsqrt(row_var + EPSILON) * ln_gain).astype(jnp.bfloat16)


def doc_positions(token_index, doc_lengths, segment_ids):
    starts = jnp.cumsum(doc_lengths) - doc_lengths
    slots = jnp.arange(doc_lengths.shape[0], dtype=jnp.int32)
    in_document = segment_ids[:, None] == slots[None, :]
    offsets = jnp.sum(jnp.where(in_document, starts[None, :], 0), axis=1)
    return token_index - offsets


def rotary(head_block, positions):
    half_rot = ROT // 2
    frequency = 10000.0 ** (-(2.0 * jnp.arange(half_rot, dtype=jnp.float32)) / ROT)
    angles = positions.astype(jnp.float32)[:, None] * frequency[None, :]
    cosine = jnp.cos(angles)[:, None, :]
    sine_part = jnp.sin(angles)[:, None, :]
    lower_half = head_block[..., :half_rot]
    upper_half = head_block[..., half_rot:ROT]
    return jnp.concatenate(
        [
            lower_half * cosine - upper_half * sine_part,
            upper_half * cosine + lower_half * sine_part,
            head_block[..., ROT:],
        ],
        axis=-1,
    )


def per_device_any(hidden_in, ln_gain, w_qkv, w_out, doc_lengths, segment_ids, pair_table, page_table):
    row_count = hidden_in.shape[0]
    whole = lax.all_gather(hidden_in, "tp", axis=1, tiled=True)
    normed = layer_norm(whole, ln_gain)
    col_count = w_qkv.shape[2]
    head_count = col_count // HD
    projected = jnp.einsum("tk,kcn->ctn", normed, w_qkv, preferred_element_type=jnp.float32)
    projected = projected.reshape(3, row_count, head_count, HD)
    block_index = lax.axis_index("blk")
    token_index = block_index * row_count + jnp.arange(row_count, dtype=jnp.int32)
    positions = doc_positions(token_index, doc_lengths, segment_ids)
    queries = rotary(projected[0], positions).astype(jnp.bfloat16)
    key_rows = rotary(projected[1], positions).astype(jnp.bfloat16)
    values = projected[2].astype(jnp.bfloat16)
    table_row = lax.dynamic_index_in_dim(pair_table, block_index, 0, keepdims=False)
    block_ids = jnp.arange(pair_table.shape[1], dtype=jnp.int32)
    scale = HD ** (-0.5)

    def attend(running, incoming, offset):
        key_piece, value_piece, segment_piece = incoming
        piece_rows = key_piece.shape[0]
        key_index = offset + jnp.arange(piece_rows, dtype=jnp.int32)
        matches = (key_index // row_count)[:, None] == block_ids[None, :]
        live = jnp.sum(jnp.where(matches, table_row[None, :], 0), axis=1) > 0

        def compute(previous):
            maxima, totals, weighted = previous
            scores = (
                jnp.einsum("qhd,khd->hqk", queries, key_piece, preferred_element_type=jnp.float32)
                * scale
            )
            allowed = (
                live[None, :]
                & (segment_ids[:, None] == segment_piece[None, :])
                & (key_index[None, :] <= token_index[:, None])
            )
            scores = jnp.where(allowed[None], scores, -jnp.inf)
            newest = jnp.maximum(maxima, jnp.max(scores, axis=-1))
            shrink = jnp.exp(maxima - newest)
            weights = jnp.exp(scores - newest[..., None])
            totals = totals * shrink + jnp.sum(weights, axis=-1)
            weighted = weighted * shrink[..., None] + jnp.einsum(
                "hqk,khd->hqd",
                weights.astype(jnp.bfloat16),
                value_piece,
                preferred_element_type=jnp.float32,
            )
            return (newest, totals, weighted)

        return lax.cond(jnp.any(live), compute, lambda previous: previous, running)

    start_state = (
        jnp.full((head_count, row_count), -1e30, jnp.float32),
        jnp.zeros((head_count, row_count), jnp.float32),
        jnp.zeros((head_count, row_count, HD), jnp.float32),
    )
    final = attend(start_state, (key_rows, values, segment_ids), block_index * row_count)
    for distance in range(1, lax.axis_size("blk") // 2 + 1):
        earlier = from_behind((key_rows, values, segment_ids), "blk", distance)
        final = attend(final, earlier, (block_index - distance) * row_count)
    mixed = (final[2] / final[1][..., None]).astype(jnp.bfloat16)
    heads_out = jnp.transpose(mixed, (1, 0, 2)).reshape(row_count, col_count)
    partial_term = jnp.dot(heads_out, w_out, preferred_element_type=jnp.float32)
    attn_out = lax.psum_scatter(
        partial_term.astype(jnp.bfloat16), "tp", scatter_dimension=1, tiled=True
    )
    page_count = row_count // PAGE
    local_pages = page_table - block_index * page_count
    stacked = jnp.stack(
        [key_rows.reshape(page_count, PAGE, col_count), values.reshape(page_count, PAGE, col_count)]
    )
    page_cache = jnp.zeros_like(stacked).at[:, local_pages].set(stacked)
    return (attn_out, page_cache)


def turn(value, distance):
    return lax.ppermute(value, "tp", [(source, (source + distance) % 4) for source in range(4)])


def line_hop(up, down, ups, downs):
    return lax.ppermute(up, "tp", ups), lax.ppermute(down, "tp", downs)


def line_owners():
    place = lax.axis_index("tp")
    first = jnp.where(place == 0, 1, place - 1)
    second = jnp.where(place == 0, 2, jnp.where(place == 3, 1, place + 1))
    third = jnp.where(place < 2, 3, 0)
    pick_second = jnp.where(place == 0, 1, jnp.where(place == 3, 2, 0))
    outer = (place == 0) | (place == 3)
    return [(place, 0 * place), (first, place == 0), (second, pick_second), (third, outer)]


def gather_line(value, work):
    up1, down1 = line_hop(value, value, [(0, 1), (1, 2), (2, 3)], [(3, 2), (2, 1), (1, 0)])
    work(0, [value])
    up2, down2 = line_hop(up1, down1, [(1, 2), (2, 3)], [(2, 1), (1, 0)])
    work(1, [up1, down1])
    inner = jnp.where(lax.axis_index("tp") == 2, up2, down2)
    outer = lax.ppermute(inner, "tp", [(2, 3), (1, 0)])
    work(2, [down1, down2, up2])
    work(3, [inner, outer])


OWNER, PICK, COLUMN, CHIP, CORE, LAST = 0, 4, 8, 12, 13, 14


def project_kernel(step, count, facts_ref, *refs):
    refs = list(refs)
    shards = refs[:count]
    mean_ref, rstd_ref, gain_ref, w_ref = refs[count : count + 4]
    del refs[: count + 4]
    previous_ref = refs.pop(0) if step > 0 else None
    kind = pl.program_id(0)
    normed_ref, turned_ref = refs[-2:]

    for pick, x_ref in enumerate(shards):

        @pl.when((kind == 0) & (facts_ref[PICK + step] == pick))
        def _():
            centred = x_ref[...].astype(jnp.float32) - mean_ref[...]
            normed_ref[...] = (centred * rstd_ref[...] * gain_ref[0]).astype(jnp.bfloat16)

    total = jnp.dot(normed_ref[...], w_ref[0], preferred_element_type=jnp.float32)
    if step > 0:
        total = total + previous_ref[0]
    if step < 3:
        refs[0][0] = total
        return
    cos_ref, sin_ref = refs[:2]
    kept_refs, given_ref = refs[2:6], refs[6]
    chip, core = facts_ref[CHIP], facts_ref[CORE]
    turned = total.T
    turned_ref[...] = turned.reshape(turned_ref.shape).astype(jnp.bfloat16)

    @pl.when(kind < 2)
    def _():
        half = ROT // 2
        for head in range(turned_ref.shape[0]):
            part = turned[head * HD : head * HD + ROT]
            swapped = jnp.concatenate([part[half:], part[:half]], axis=0)
            turned_ref[head, :ROT] = (part * cos_ref[...] + swapped * sin_ref[...]).astype(jnp.bfloat16)

    for distance in range(4):
        head = 2 * (chip ^ distance)
        kept_refs[distance][...] = turned_ref[head + core]
        given_ref[distance] = turned_ref[head + 1 - core]


def project(step, facts, shards, mean, rstd, gain, w3, previous, tables):
    rows, depth = shards[0].shape
    width = w3.shape[2]
    column = pl.BlockSpec((rows, 1), lambda c, o: (0, 0))
    in_specs = [pl.BlockSpec((rows, depth), lambda c, o: (0, 0)) for _ in shards] + [
        column,
        column,
        pl.BlockSpec((1, 1, depth), lambda c, o: (o[OWNER + step], 0, 0)),
        pl.BlockSpec((1, depth, width), lambda c, o: (c, o[OWNER + step], 0)),
    ]
    args = [*shards, mean, rstd, gain, w3]
    sums = pl.BlockSpec((1, rows, width), lambda c, o: (c, 0, 0))
    if step > 0:
        in_specs.append(sums)
        args.append(previous)
    out_shape, out_specs = jax.ShapeDtypeStruct((3, rows, width), jnp.float32), sums
    if step == 3:
        in_specs += [pl.BlockSpec((ROT, rows), lambda c, o: (0, 0))] * 2
        args += tables
        out_shape = [jax.ShapeDtypeStruct((3 * HD, rows), jnp.bfloat16)] * 4
        out_shape.append(jax.ShapeDtypeStruct((4, 3 * HD, rows), jnp.bfloat16))
        out_specs = [pl.BlockSpec((HD, rows), lambda c, o: (c, 0))] * 4
        out_specs.append(pl.BlockSpec((4, HD, rows), lambda c, o: (0, c, 0)))
    return pl.pallas_call(
        functools.partial(project_kernel, step, len(shards)),
        grid_spec=pltpu.PrefetchScalarGridSpec(
            num_scalar_prefetch=1,
            grid=(3,),
            in_specs=in_specs,
            out_specs=out_specs,
            scratch_shapes=[
                pltpu.VMEM((rows, depth), jnp.bfloat16),
                pltpu.VMEM((width // HD, HD, rows), jnp.bfloat16),
            ],
        ),
        out_shape=out_shape,
        compiler_params=pltpu.CompilerParams(vmem_limit_bytes=48 << 20),
        cost_estimate=pl.CostEstimate(
            flops=24 * rows * depth * width, bytes_accessed=6 * depth * width, transcendentals=0
        ),
        name="project",
    )(facts, *args)


def attend_kernel(facts_ref, pair_ref, start_ref, *refs):
    pieces, outs, (q_ref, k_ref, v_ref, top_ref, sum_ref, acc_ref) = refs[:-10], refs[-10:-6], refs[-6:]
    chip, own_core = facts_ref[CHIP], facts_ref[CORE]
    rows = q_ref.shape[2]
    for distance in range(4):
        for other, piece in enumerate(pieces[2 * distance : 2 * distance + 2]):
            block = 2 * (chip ^ distance) + (own_core ^ other)
            q_ref[block] = piece[:HD]
            k_ref[block] = piece[HD : 2 * HD].T
            v_ref[block] = piece[2 * HD :]
    scale = HD ** (-0.5) * 1.4426950408889634

    def one_block(block, carry):
        token = block * rows + lax.broadcasted_iota(jnp.int32, (1, rows), 1)
        start = start_ref[block]
        top_ref[...] = jnp.full_like(top_ref, -1e30)
        sum_ref[...] = jnp.zeros_like(sum_ref)
        acc_ref[...] = jnp.zeros_like(acc_ref)

        def update(other, masked):
            scores = jnp.dot(k_ref[other], q_ref[block], preferred_element_type=jnp.float32) * scale
            if masked:
                key = other * rows + lax.broadcasted_iota(jnp.int32, (rows, rows), 0)
                scores = jnp.where((key >= start) & (key <= token), scores, -jnp.inf)
            newest = jnp.maximum(top_ref[...], jnp.max(scores, axis=0, keepdims=True))
            shrink = jnp.exp2(top_ref[...] - newest)
            weights = jnp.exp2(scores - newest)
            top_ref[...] = newest
            sum_ref[...] = sum_ref[...] * shrink + jnp.sum(weights, axis=0, keepdims=True)
            acc_ref[...] = acc_ref[...] * shrink + jnp.dot(
                v_ref[other], weights.astype(jnp.bfloat16), preferred_element_type=jnp.float32
            )

        def one_pair(other, inner):
            live = pair_ref[block, other] > 0
            whole = facts_ref[LAST + block] <= other * rows

            @pl.when(live & whole & (other < block))
            def _():
                update(other, False)

            @pl.when(live & ~(whole & (other < block)))
            def _():
                update(other, True)

            return inner

        lax.fori_loop(0, block + 1, one_pair, 0)
        mixed = (acc_ref[...] / sum_ref[...]).astype(jnp.bfloat16)
        for distance, out_ref in enumerate(outs):

            @pl.when((block // 2) ^ chip == distance)
            def _():
                out_ref[block % 2] = mixed

        return carry

    lax.fori_loop(0, q_ref.shape[0], one_block, 0)


def attend(facts, pair_table, start, pieces):
    blocks, _, rows = start.shape
    smem = pl.BlockSpec(memory_space=pltpu.SMEM)
    vmem = pl.BlockSpec(memory_space=pltpu.VMEM)
    return pl.pallas_call(
        attend_kernel,
        in_specs=[smem, smem, vmem] + [vmem] * len(pieces),
        out_specs=[vmem] * 4,
        out_shape=[jax.ShapeDtypeStruct((2, HD, rows), jnp.bfloat16)] * 4,
        scratch_shapes=[
            pltpu.VMEM((blocks, HD, rows), jnp.bfloat16),
            pltpu.VMEM((blocks, rows, HD), jnp.bfloat16),
            pltpu.VMEM((blocks, HD, rows), jnp.bfloat16),
            pltpu.VMEM((1, rows), jnp.float32),
            pltpu.VMEM((1, rows), jnp.float32),
            pltpu.VMEM((HD, rows), jnp.float32),
        ],
        compiler_params=pltpu.CompilerParams(vmem_limit_bytes=28 << 20),
        cost_estimate=pl.CostEstimate(flops=1000, bytes_accessed=1000, transcendentals=0),
        name="attend",
    )(facts, pair_table, start, *pieces)


def swap(value, distance):
    count = lax.axis_size("blk")
    return lax.ppermute(value, "blk", [(place, place ^ distance) for place in range(count)])


def to_heads(kept, got):
    pieces = []
    for distance in range(4):
        for value in (kept[distance], got[distance]):
            pieces.append(value if distance == 0 else swap(value, 2 * distance))
    return pieces


def order_kernel(facts_ref, *refs):
    pairs, got_ref, out_ref = refs[:4], refs[4], refs[5]
    chip, core = facts_ref[CHIP], facts_ref[CORE]
    for distance in range(4):
        head = 2 * (chip ^ distance)
        out_ref[head + core] = pairs[distance][core]
        out_ref[head + 1 - core] = got_ref[distance]


def to_blocks(facts, mixed):
    core = lax.axis_index("blk") % 2
    held = [pair if distance == 0 else swap(pair, 2 * distance) for distance, pair in enumerate(mixed)]
    given = [lax.dynamic_index_in_dim(pair, 1 - core, 0, keepdims=False) for pair in held]
    got = swap(jnp.stack(given), 1)
    vmem = pl.BlockSpec(memory_space=pltpu.VMEM)
    heads = pl.pallas_call(
        order_kernel,
        in_specs=[pl.BlockSpec(memory_space=pltpu.SMEM)] + [vmem] * 5,
        out_specs=vmem,
        out_shape=jax.ShapeDtypeStruct((8,) + got.shape[1:], got.dtype),
        cost_estimate=pl.CostEstimate(flops=0, bytes_accessed=2 << 20, transcendentals=0),
        name="order",
    )(facts, *held, got)
    return heads.reshape((8 * HD,) + got.shape[2:])


def combine_kernel(steps, counts, facts_ref, *refs):
    refs = list(refs)
    arrays = []
    for count in counts:
        arrays.append(refs[:count])
        del refs[:count]
    own_ref, others_ref = (refs.pop(0) if 0 in steps else None), refs.pop(0)
    previous_ref = refs.pop(0) if 0 not in steps else None
    out_ref, sum_ref = refs
    slot = pl.program_id(1)
    for place, step in enumerate(steps):
        for pick, h_ref in enumerate(arrays[place]):

            @pl.when((slot == place) & (facts_ref[PICK + step] == pick))
            def _():
                w_ref = own_ref if step == 0 else others_ref
                product = lax.dot_general(
                    h_ref[...],
                    w_ref[...].reshape(h_ref.shape[0], out_ref.shape[1]),
                    (((0,), (0,)), ((), ())),
                    preferred_element_type=jnp.float32,
                )
                if place > 0:
                    product = product + sum_ref[...]
                elif previous_ref is not None:
                    product = product + previous_ref[...].astype(jnp.float32)
                if place < len(steps) - 1:
                    sum_ref[...] = product
                else:
                    out_ref[...] = product.astype(out_ref.dtype)


def combine(steps, facts, arrays, own, others, previous=None):
    depth, rows = arrays[-1][-1].shape
    outer, _, inner, width = others.shape
    tile = width // 2
    out_spec = pl.BlockSpec((rows, tile), lambda n, k, o: (0, n))
    in_specs = [pl.BlockSpec((depth, rows), lambda n, k, o: (0, 0)) for step in arrays for _ in step]
    args = [array for step in arrays for array in step]
    if 0 in steps:
        in_specs.append(pl.BlockSpec((1, 1, depth, tile), lambda n, k, o: (0, 0, 0, n)))
        args.append(own)
    in_specs.append(
        pl.BlockSpec((outer, 1, inner, tile), lambda n, k, o: (0, o[COLUMN + steps[0] + k], 0, n))
    )
    args.append(others)
    if 0 not in steps:
        in_specs.append(out_spec)
        args.append(previous)
    return pl.pallas_call(
        functools.partial(combine_kernel, steps, tuple(len(step) for step in arrays)),
        grid_spec=pltpu.PrefetchScalarGridSpec(
            num_scalar_prefetch=1,
            grid=(width // tile, len(steps)),
            in_specs=in_specs,
            out_specs=out_spec,
            scratch_shapes=[pltpu.VMEM((rows, tile), jnp.float32)],
        ),
        out_shape=jax.ShapeDtypeStruct((rows, width), jnp.bfloat16),
        compiler_params=pltpu.CompilerParams(vmem_limit_bytes=56 << 20),
        cost_estimate=pl.CostEstimate(
            flops=4 * len(steps) * rows * depth * width,
            bytes_accessed=2 * len(steps) * depth * width,
            transcendentals=0,
        ),
        name="combine",
    )(facts, *args)


def share_kernel(facts_ref, w_ref, *refs):
    outs, sems = refs[-4:-1], refs[-1]
    rows, width = outs[0].shape
    first = facts_ref[0] * rows
    copies = []
    for place, out_ref in enumerate(outs):
        begin = pl.multiple_of(facts_ref[1 + place] * width, width)
        window = w_ref.at[pl.ds(pl.multiple_of(first, rows), rows), pl.ds(begin, width)]
        copies.append(pltpu.make_async_copy(window, out_ref, sems.at[place]))
    for copy in copies:
        copy.start()
    for copy in copies:
        copy.wait()


def shares(numbers, w_out, width, waited):
    any_space = pl.BlockSpec(memory_space=pl.ANY)
    return pl.pallas_call(
        share_kernel,
        in_specs=[pl.BlockSpec(memory_space=pltpu.SMEM), any_space] + [any_space] * len(waited),
        out_specs=[pl.BlockSpec(memory_space=pltpu.VMEM)] * 3,
        out_shape=[jax.ShapeDtypeStruct((HD, width), w_out.dtype)] * 3,
        scratch_shapes=[pltpu.SemaphoreType.DMA((3,))],
        cost_estimate=pl.CostEstimate(flops=0, bytes_accessed=2 << 20, transcendentals=0),
        name="shares",
    )(numbers, w_out, *waited)


def stack_kernel(*refs):
    for place in range(3):
        refs[-1][place] = refs[place][...]


def stack(values, waited):
    any_space, vmem = pl.BlockSpec(memory_space=pl.ANY), pl.BlockSpec(memory_space=pltpu.VMEM)
    return pl.pallas_call(
        stack_kernel,
        in_specs=[vmem] * 3 + [any_space] * len(waited),
        out_specs=vmem,
        out_shape=jax.ShapeDtypeStruct((3,) + values[0].shape, values[0].dtype),
        cost_estimate=pl.CostEstimate(flops=0, bytes_accessed=2 << 20, transcendentals=0),
        name="stack",
    )(*values, *waited)


def pages_kernel(facts_ref, *refs):
    kept_refs, given_ref, out_ref, turned_ref = refs[:4], refs[4], refs[5], refs[6]
    blocks = facts_ref.shape[0] - LAST - out_ref.shape[1]
    chip, core = facts_ref[CHIP], facts_ref[CORE]
    for tile in range(given_ref.shape[2] // 128):
        tokens = slice(tile * 128, (tile + 1) * 128)
        for kind in range(2):
            entries = slice((kind + 1) * HD, (kind + 2) * HD)
            for distance in range(4):
                head = 2 * (chip ^ distance)
                turned_ref[head + core] = kept_refs[distance][entries, tokens]
                turned_ref[head + 1 - core] = given_ref[distance, entries, tokens]
            turned = turned_ref[...].reshape(8 * HD, 128).T
            for page in range(128 // PAGE):
                place = facts_ref[LAST + blocks + tile * 128 // PAGE + page]
                out_ref[kind, place] = turned[page * PAGE : (page + 1) * PAGE]


def pages(facts, count, parts):
    width = 8 * HD
    vmem = pl.BlockSpec(memory_space=pltpu.VMEM)
    return pl.pallas_call(
        pages_kernel,
        in_specs=[pl.BlockSpec(memory_space=pltpu.SMEM)] + [vmem] * len(parts),
        out_specs=vmem,
        scratch_shapes=[pltpu.VMEM((8, HD, 128), jnp.bfloat16)],
        out_shape=jax.ShapeDtypeStruct((2, count, PAGE, width), jnp.bfloat16),
        compiler_params=pltpu.CompilerParams(vmem_limit_bytes=56 << 20),
        cost_estimate=pl.CostEstimate(flops=0, bytes_accessed=10 << 20, transcendentals=0),
        name="pages",
    )(facts, *parts)


def per_device_heads(hidden_in, ln_gain, w_qkv, w_out, doc_lengths, segment_ids, pair_table, page_table):
    rows, depth = hidden_in.shape
    width = w_qkv.shape[2]
    block, place = lax.axis_index("blk"), lax.axis_index("tp")
    chip = block // 2
    blocks = lax.axis_size("blk")
    values32 = hidden_in.astype(jnp.float32)
    own_mean = jnp.mean(values32, axis=1)
    own_square = jnp.mean((values32 - own_mean[:, None]) ** 2, axis=1)
    own_stats = jnp.stack([own_mean, own_square])
    stats = jnp.stack([own_stats] + [turn(own_stats, distance) for distance in (1, 2, 3)])
    mean = jnp.mean(stats[:, 0], axis=0)
    variance = jnp.mean(stats[:, 1] + (stats[:, 0] - mean[None]) ** 2, axis=0)
    rstd = lax.rsqrt(variance + EPSILON)[:, None]
    mean = mean[:, None]
    gain = ln_gain.reshape(4, 1, depth)
    w3 = jnp.transpose(w_qkv, (1, 0, 2))

    token_index = block * rows + jnp.arange(rows, dtype=jnp.int32)
    positions = doc_positions(token_index, doc_lengths, segment_ids)
    frequency = 10000.0 ** (-(2.0 * jnp.arange(ROT // 2, dtype=jnp.float32)) / ROT)
    angles = positions.astype(jnp.float32)[None, :] * frequency[:, None]
    cosine, sine = jnp.cos(angles), jnp.sin(angles)
    cosine = jnp.concatenate([cosine, cosine])
    sine = jnp.concatenate([-sine, sine])

    ends = jnp.cumsum(doc_lengths)
    tokens = jnp.arange(blocks * rows, dtype=jnp.int32)
    start = jnp.max(jnp.where(ends[:, None] <= tokens[None, :], ends[:, None], 0), axis=0)
    start = start.astype(jnp.int32).reshape(blocks, 1, rows)
    page_count = rows // PAGE
    steps = line_owners()
    numbers = [owner for owner, _ in steps] + [pick for _, pick in steps]
    numbers += [jnp.maximum((place - owner) % 4 - 1, 0) for owner, _ in steps] + [chip, block % 2]
    facts = jnp.concatenate(
        [
            jnp.stack([jnp.asarray(number).astype(jnp.int32) for number in numbers]),
            start[:, 0, rows - 1],
            page_table - block * page_count,
        ]
    )

    total = [None]

    def take_in(step, arrays):
        total[0] = project(
            step, facts, arrays, mean, rstd, gain, w3, total[0], [cosine, sine]
        )

    gather_line(hidden_in, take_in)
    *kept, given = total[0]
    arrived = to_heads(kept, swap(given, 1))
    page_cache = pages(facts, page_count, [*kept, given])

    windows = jnp.stack([block] + [(place + distance) % 4 for distance in (1, 2, 3)]).astype(jnp.int32)
    windows = shares(windows, w_out, depth, [arrived[5], arrived[7]])
    columns = [turn(window, distance) for distance, window in zip((1, 2, 3), windows)]
    mixed = attend(facts, pair_table, start, arrived)
    others = lax.all_gather(stack(columns, mixed[:1]), "blk", axis=0)
    heads = to_blocks(facts, mixed)
    own = lax.dynamic_slice_in_dim(w_out, place * depth, depth, 1).reshape(1, 1, width, depth)

    came, result = [], [None]

    def add_in(step, arrays):
        came.append(arrays)
        if step == 2:
            result[0] = combine((0, 1, 2), facts, came[:3], own, others)
        if step == 3:
            result[0] = combine((3,), facts, came[3:], own, others, result[0])

    gather_line(heads, add_in)
    attn_out = result[0]
    return (attn_out, page_cache)


def solution(mesh):
    placed = (P("blk", "tp"), P(), P(None, None, "tp"), P("tp", None), P(), P("blk"), P(), P("blk"))

    def per_device(hidden_in, ln_gain, w_qkv, *rest):
        heads = w_qkv.shape[2] // HD
        fits = mesh.shape["tp"] == 4 and mesh.shape["blk"] == 8 and heads == 8
        form = per_device_heads if fits else per_device_any
        return form(hidden_in, ln_gain, w_qkv, *rest)

    return jax.shard_map(
        per_device,
        mesh=mesh,
        in_specs=placed,
        out_specs=(P("blk", "tp"), P(None, "blk", None, "tp")),
        check_vma=False,
    )
```

profile of v0, /device:TPU:0, one launch (start us, length us, event | category | flops | bytes accessed | tf_op | source)
XLA Modules:
  0.0 298.2 jit_solution(4826604763043093970)
XLA Ops:
  7.2 1.8 convert_reduce_fusion
  9.6 3.1 %collective-permute-start.5 = (f32[2,512]{1,0:T(2,128)S(1)}, f32[2,512]{1,0:T(2,128)S(1)}, u32[]{:S(2)}, u32[]{:S(2)}) collective-permute-start(f32[2,512]{1,0:T(2,128)S(1)} %get-tuple-element.31), channel_id=1, source_target_pairs={{0,1},{1,2},{2,3},{3,0},{4,5},{5,6},{6,7},{7,4},{8,9},{9,10},{10,1... | collective-permute-start | bytes 12296 | tf_op jit(solution)/shard_map/ppermute | solution.py:134
  12.7 2.6 collective-permute-start.6
  15.3 1.3 collective-permute-start.7
  16.7 1.3 collective-permute-start.2
  18.0 5.8 %collective-permute-start = (bf16[512,1536]{1,0:T(8,128)(2,1)S(1)}, bf16[512,1536]{1,0:T(8,128)(2,1)}, u32[]{:S(2)}, u32[]{:S(2)}) collective-permute-start(bf16[512,1536]{1,0:T(8,128)(2,1)S(1)} %copy-done), channel_id=1, source_target_pairs={{0,1},{1,2},{2,3},{4,5},{5,6},{6,7},{8,9},{9,10},{10,11},{12,13},{... | collective-permute-start | bytes 4718600 | tf_op jit(solution)/shard_map/ppermute | solution.py:138
  25.3 28.7 %collective-permute-done.2.refs_1_.refs_0_ = bf16[512,1536]{1,0:T(8,128)(2,1)} collective-permute-done((bf16[512,1536]{1,0:T(8,128)(2,1)S(1)}, bf16[512,1536]{1,0:T(8,128)(2,1)}, u32[]{:S(2)}, u32[]{:S(2)}) %collective-permute-start.2) | collective-permute-done | bytes 1572896 | tf_op jit(solution)/shard_map/ppermute | solution.py:138
  53.9 1.3 collective-permute-start.3
  55.2 1.8 collective-permute-start.1
  59.4 0.9 copy-done.14
  60.3 9.0 %project.4.refs_6_ = f32[3,512,768]{2,1,0:T(8,128)} custom-call(s32[54]{0:T(128)S(1)} %concatenate.9.facts_ref, bf16[512,1536]{1,0:T(8,128)(2,1)S(1)} %copy-done, f32[512,1]{1,0:T(8,128)S(1)} %copy-done.14, f32[512,1]{1,0:T(8,128)S(1)} %copy.43.refs_2_.refs_3_.refs_4_, f32[4,1,1536]{2,1,0:T(1,128)S(1)} %bitcast.54, bf16[3,6144,768]{2,1,0:T(8,128)(2,1)} %bitcast.70), custom_call_target="tpu_custom_call" | custom-call | flops 14495514624 | bytes 7077888 | tf_op jit(solution)/shard_map/project/pallas_call | solution.py:230
  69.4 21.0 %collective-permute-done.3.refs_1_ = bf16[512,1536]{1,0:T(8,128)(2,1)S(1)} collective-permute-done((bf16[512,1536]{1,0:T(8,128)(2,1)}, bf16[512,1536]{1,0:T(8,128)(2,1)S(1)}, u32[]{:S(2)}, u32[]{:S(2)}) %collective-permute-start.3) | collective-permute-done | bytes 1572896 | tf_op jit(solution)/shard_map/ppermute | solution.py:138
  90.7 1.5 collective-permute-start.4
  92.2 11.4 %project.5.refs_7_ = f32[3,512,768]{2,1,0:T(8,128)} custom-call(s32[54]{0:T(128)S(1)} %concatenate.9.facts_ref, bf16[512,1536]{1,0:T(8,128)(2,1)} %collective-permute-done.refs_0_, bf16[512,1536]{1,0:T(8,128)(2,1)} %collective-permute-done.2.refs_1_.refs_0_, f32[512,1]{1,0:T(8,128)S(1)} %copy-done.14, f32[512,1]{1,0:T(8,128)S(1)} %copy.43.refs_2_.refs_3_.refs_4_, ...), custom_call_target="tpu_custom_call" | custom-call | flops 14495514624 | bytes 7077888 | tf_op jit(solution)/shard_map/project/pallas_call | solution.py:230
  103.7 11.5 %project.6.refs_6_ = f32[3,512,768]{2,1,0:T(8,128)} custom-call(s32[54]{0:T(128)S(1)} %concatenate.9.facts_ref, bf16[512,1536]{1,0:T(8,128)(2,1)} %collective-permute-done.2.refs_1_.refs_0_, bf16[512,1536]{1,0:T(8,128)(2,1)S(1)} %collective-permute-done.3.refs_1_, bf16[512,1536]{1,0:T(8,128)(2,1)} %collective-permute-done.1.refs_2_, ...), custom_call_target="tpu_custom_call" | custom-call | flops 14495514624 | bytes 7077888 | tf_op jit(solution)/shard_map/project/pallas_call | solution.py:230
  115.2 10.9 %collective-permute-done.4.refs_1_ = bf16[512,1536]{1,0:T(8,128)(2,1)S(1)} collective-permute-done((bf16[512,1536]{1,0:T(8,128)(2,1)S(1)}, bf16[512,1536]{1,0:T(8,128)(2,1)S(1)}, u32[]{:S(2)}, u32[]{:S(2)}) %collective-permute-start.4) | collective-permute-done | bytes 1572896 | tf_op jit(solution)/shard_map/ppermute | solution.py:157
  126.1 0.9 copy-done.13
  127.6 8.8 %project.7 = (bf16[288,512]{1,0:T(8,128)(2,1)S(1)}, bf16[288,512]{1,0:T(8,128)(2,1)S(1)}, bf16[288,512]{1,0:T(8,128)(2,1)S(1)}, bf16[288,512]{1,0:T(8,128)(2,1)S(1)}, bf16[4,288,512]{2,1,0:T(8,128)(2,1)S(1)}) custom-call(s32[54]{0:T(128)S(1)} %copy-done.16, bf16[512,1536]{1,0:T(8,128)(2,1)S(1)} %broadcast_select_fusion.refs_0_, ...), custom_call_target="tpu_custom_call" | custom-call | flops 14495514624 | bytes 7077888 | tf_op jit(solution)/shard_map/project/pallas_call | solution.py:230
  136.6 2.8 collective-permute-done.8
  140.4 1.5 collective-permute-start.12
  141.9 1.4 collective-permute-start.14
  143.3 1.5 collective-permute-start.11
  145.9 1.5 collective-permute-start.9
  147.4 15.7 %collective-permute-done.12.refs_5_.refs_0_ = bf16[288,512]{1,0:T(8,128)(2,1)S(1)} collective-permute-done((bf16[288,512]{1,0:T(8,128)(2,1)}, bf16[288,512]{1,0:T(8,128)(2,1)S(1)}, u32[]{:S(2)}, u32[]{:S(2)}) %collective-permute-start.12) | collective-permute-done | bytes 294944 | tf_op jit(solution)/shard_map/ppermute | solution.py:336
  163.1 1.5 collective-permute-start.10
  165.3 2.8 shares.1
  168.7 4.6 %collective-permute-start.25 = (bf16[96,1536]{1,0:T(8,128)(2,1)}, bf16[96,1536]{1,0:T(8,128)(2,1)S(1)}, u32[]{:S(2)}, u32[]{:S(2)}) collective-permute-start(bf16[96,1536]{1,0:T(8,128)(2,1)} %get-tuple-element.24), channel_id=1, source_target_pairs={{0,2},{1,3},{2,0},{3,1},{4,6},{5,7},{6,4},{7,5},{8,10},{9,11},{10,... | collective-permute-start | bytes 884744 | tf_op jit(solution)/shard_map/ppermute | solution.py:134
  173.8 1.0 copy-done.5
  174.7 1.0 copy-done.7
  175.7 17.7 %attend.1 = (bf16[2,96,512]{2,1,0:T(8,128)(2,1)S(1)}, bf16[2,96,512]{2,1,0:T(8,128)(2,1)S(1)}, bf16[2,96,512]{2,1,0:T(8,128)(2,1)S(1)}, bf16[2,96,512]{2,1,0:T(8,128)(2,1)S(1)}) custom-call(s32[54]{0:T(128)S(1)} %copy-done.17, s32[8,8]{1,0:T(8,128)S(1)} %copy-done.18, s32[8,1,512]{2,1,0:T(1,128)S(1)} %bitcast.53, ...), custom_call_target="tpu_custom_call" | custom-call | flops 1000 | bytes 1000 | tf_op jit(solution)/shard_map/attend/pallas_call | solution.py:315
  195.0 2.1 stack.114
  197.2 2.0 collective-permute-start.17
  199.7 1.0 collective-permute-start.15
  200.8 5.2 %collective-permute-done.17.refs_3_ = bf16[2,96,512]{2,1,0:T(8,128)(2,1)S(1)} collective-permute-done((bf16[2,96,512]{2,1,0:T(8,128)(2,1)S(1)}, bf16[2,96,512]{2,1,0:T(8,128)(2,1)S(1)}, u32[]{:S(2)}, u32[]{:S(2)}) %collective-permute-start.17) | collective-permute-done | bytes 196640 | tf_op jit(solution)/shard_map/ppermute | solution.py:336
  205.9 2.0 collective-permute-done.16.refs_2_
  208.2 1.7 collective-permute-done.18.refs_4_
  210.7 2.3 order.1
  213.0 10.4 %collective-permute-start.19 = (bf16[768,512]{1,0:T(8,128)(2,1)}, bf16[768,512]{1,0:T(8,128)(2,1)S(1)}, u32[]{:S(2)}, u32[]{:S(2)}) collective-permute-start(bf16[768,512]{1,0:T(8,128)(2,1)} %bitcast.60), channel_id=1, source_target_pairs={{0,1},{1,2},{2,3},{4,5},{5,6},{6,7},{8,9},{9,10},{10,11},{12,13},{... | collective-permute-start | bytes 2359304 | tf_op jit(solution)/shard_map/ppermute | solution.py:138
  223.4 1.3 collective-permute-start.21
  224.7 16.1 %collective-permute-done.19.refs_1_ = bf16[768,512]{1,0:T(8,128)(2,1)S(1)} collective-permute-done((bf16[768,512]{1,0:T(8,128)(2,1)}, bf16[768,512]{1,0:T(8,128)(2,1)S(1)}, u32[]{:S(2)}, u32[]{:S(2)}) %collective-permute-start.19) | collective-permute-done | bytes 786464 | tf_op jit(solution)/shard_map/ppermute | solution.py:138
  241.5 3.3 %collective-permute-done.21.refs_2_.refs_3_ = bf16[768,512]{1,0:T(8,128)(2,1)S(1)} collective-permute-done((bf16[768,512]{1,0:T(8,128)(2,1)}, bf16[768,512]{1,0:T(8,128)(2,1)S(1)}, u32[]{:S(2)}, u32[]{:S(2)}) %collective-permute-start.21) | collective-permute-done | bytes 786464 | tf_op jit(solution)/shard_map/ppermute | solution.py:138
  244.8 1.3 collective-permute-start.22
  246.2 19.1 %collective-permute-done.22.refs_4_ = bf16[768,512]{1,0:T(8,128)(2,1)S(1)} collective-permute-done((bf16[768,512]{1,0:T(8,128)(2,1)S(1)}, bf16[768,512]{1,0:T(8,128)(2,1)S(1)}, u32[]{:S(2)}, u32[]{:S(2)}) %collective-permute-start.22) | collective-permute-done | bytes 786464 | tf_op jit(solution)/shard_map/ppermute | solution.py:138
  265.4 1.5 collective-permute-start.23
  266.9 3.3 %dynamic-slice_bitcast_fusion.refs_6_ = bf16[1,1,768,1536]{3,2,1,0:T(8,128)(2,1)} fusion(bf16[768,6144]{1,0:T(8,128)(2,1)} %w_ref.1, s32[]{:T(128)S(6)} %select_n.115), kind=kLoop, calls=%fused_computation.4 | loop fusion | bytes 4718596 | tf_op jit(solution)/shard_map/reshape | solution.py:580
  270.2 3.3 %pages.1 = bf16[2,32,16,768]{3,2,1,0:T(8,128)(2,1)} custom-call(s32[54]{0:T(128)} %copy-done.15, bf16[288,512]{1,0:T(8,128)(2,1)} %copy-done.3, bf16[288,512]{1,0:T(8,128)(2,1)} %copy-done.9, bf16[288,512]{1,0:T(8,128)(2,1)} %copy-done.10, bf16[288,512]{1,0:T(8,128)(2,1)} %copy-done.11, bf16[4,288,512]{2,1,0:T(8,128)(2,1)} %copy-done.8), custom_call_target="tpu_custom_call" | custom-call | bytes 10485760 | tf_op jit(solution)/shard_map/pages/pallas_call | solution.py:508
  273.5 11.6 %combine.2.refs_3_ = bf16[512,1536]{1,0:T(8,128)(2,1)} custom-call(s32[54]{0:T(128)} %copy-done.15, bf16[768,512]{1,0:T(8,128)(2,1)} %bitcast.62, bf16[768,512]{1,0:T(8,128)(2,1)} %copy-done.34, bf16[768,512]{1,0:T(8,128)(2,1)} %copy-done.35, bf16[768,512]{1,0:T(8,128)(2,1)} %copy-done.35, bf16[768,512]{1,0:T(8,128)(2,1)} %copy-done.23, ...), custom_call_target="tpu_custom_call" | custom-call | flops 7247757312 | bytes 7077888 | tf_op jit(solution)/shard_map/combine/pallas_call | solution.py:422
  286.1 5.2 %combine.3 = bf16[512,1536]{1,0:T(8,128)(2,1)} custom-call(s32[54]{0:T(128)} %copy-done.15, bf16[768,512]{1,0:T(8,128)(2,1)} %copy-done.21, bf16[768,512]{1,0:T(8,128)(2,1)} %copy-done.24, bf16[8,3,96,1536]{3,2,1,0:T(8,128)(2,1)} %bitcast.59, bf16[512,1536]{1,0:T(8,128)(2,1)} %combine.2.refs_3_), custom_call_target="tpu_custom_call" | custom-call | flops 2415919104 | bytes 2359296 | tf_op jit(solution)/shard_map/combine/pallas_call | solution.py:422
  (133 shorter events, 13.7 us)
Async XLA Ops:
  7.2 16.6 %copy-start.33 = (s32[32]{0:T(128)S(1)}, s32[32]{0:T(128)}, u32[]{:S(2)}) copy-start(s32[32]{0:T(128)} %param.12) | copy-start | bytes 388
  7.2 17.3 %copy-start.32 = (s32[512]{0:T(512)S(1)}, s32[512]{0:T(512)}, u32[]{:S(2)}) copy-start(s32[512]{0:T(512)} %param.13) | copy-start | bytes 6148
  7.2 17.7 %copy-start.36 = (s32[32]{0:T(128)S(1)}, s32[32]{0:T(128)}, u32[]{:S(2)}) copy-start(s32[32]{0:T(128)} %param.15) | copy-start | bytes 388
  7.2 266.3 %all-gather.3.cloned.1.call-start = ((), (), s32[]{:S(2)}) async-start(), calls=%async_computation | async-start | bytes 7962624 | tf_op jit(solution)/shard_map/all_gather | solution.py:578
  9.0 50.3 %copy-start.19 = (f32[6144]{0:T(1024)S(1)}, f32[6144]{0:T(1024)}, u32[]{:S(2)}) copy-start(f32[6144]{0:T(1024)} %param.9) | copy-start | bytes 73732
  9.6 15.5 %collective-permute-start.5 = (f32[2,512]{1,0:T(2,128)S(1)}, f32[2,512]{1,0:T(2,128)S(1)}, u32[]{:S(2)}, u32[]{:S(2)}) collective-permute-start(f32[2,512]{1,0:T(2,128)S(1)} %get-tuple-element.31), channel_id=1, source_target_pairs={{0,1},{1,2},{2,3},{3,0},{4,5},{5,6},{6,7},{7,4},{8,9},{9,10},{10,1... | collective-permute-start | bytes 12296 | tf_op jit(solution)/shard_map/ppermute | solution.py:134
  12.7 12.4 %collective-permute-start.6 = (f32[2,512]{1,0:T(2,128)S(1)}, f32[2,512]{1,0:T(2,128)S(1)}, u32[]{:S(2)}, u32[]{:S(2)}) collective-permute-start(f32[2,512]{1,0:T(2,128)S(1)} %get-tuple-element.31), channel_id=1, source_target_pairs={{0,2},{1,3},{2,0},{3,1},{4,6},{5,7},{6,4},{7,5},{8,10},{9,11},{10,... | collective-permute-start | bytes 12296 | tf_op jit(solution)/shard_map/ppermute | solution.py:134
  15.3 9.9 %collective-permute-start.7 = (f32[2,512]{1,0:T(2,128)S(1)}, f32[2,512]{1,0:T(2,128)S(1)}, u32[]{:S(2)}, u32[]{:S(2)}) collective-permute-start(f32[2,512]{1,0:T(2,128)S(1)} %get-tuple-element.31), channel_id=1, source_target_pairs={{0,3},{1,0},{2,1},{3,2},{4,7},{5,4},{6,5},{7,6},{8,11},{9,8},{10,9... | collective-permute-start | bytes 12296 | tf_op jit(solution)/shard_map/ppermute | solution.py:134
  16.7 37.3 %collective-permute-start.2 = (bf16[512,1536]{1,0:T(8,128)(2,1)S(1)}, bf16[512,1536]{1,0:T(8,128)(2,1)}, u32[]{:S(2)}, u32[]{:S(2)}) collective-permute-start(bf16[512,1536]{1,0:T(8,128)(2,1)S(1)} %copy-done), channel_id=1, source_target_pairs={{3,2},{2,1},{1,0},{7,6},{6,5},{5,4},{11,10},{10,9},{9,8},{15,14},{... | collective-permute-start | bytes 4718600 | tf_op jit(solution)/shard_map/ppermute | solution.py:138
  18.0 37.3 %collective-permute-start = (bf16[512,1536]{1,0:T(8,128)(2,1)S(1)}, bf16[512,1536]{1,0:T(8,128)(2,1)}, u32[]{:S(2)}, u32[]{:S(2)}) collective-permute-start(bf16[512,1536]{1,0:T(8,128)(2,1)S(1)} %copy-done), channel_id=1, source_target_pairs={{0,1},{1,2},{2,3},{4,5},{5,6},{6,7},{8,9},{9,10},{10,11},{12,13},{... | collective-permute-start | bytes 4718600 | tf_op jit(solution)/shard_map/ppermute | solution.py:138
  25.1 78.5 %copy-start.15 = (s32[54]{0:T(128)}, s32[54]{0:T(128)S(1)}, u32[]{:S(2)}) copy-start(s32[54]{0:T(128)S(1)} %concatenate.9.facts_ref) | copy-start | bytes 652
  53.9 36.5 %collective-permute-start.3 = (bf16[512,1536]{1,0:T(8,128)(2,1)}, bf16[512,1536]{1,0:T(8,128)(2,1)S(1)}, u32[]{:S(2)}, u32[]{:S(2)}) collective-permute-start(bf16[512,1536]{1,0:T(8,128)(2,1)} %collective-permute-done.2.refs_1_.refs_0_), channel_id=1, source_target_pairs={{2,1},{1,0},{6,5},{5,4},{10,9},{9,8},{14,13},{13,12},{18,17},{17,1... | collective-permute-start | bytes 4718600 | tf_op jit(solution)/shard_map/ppermute | solution.py:138
  55.2 35.2 %collective-permute-start.1 = (bf16[512,1536]{1,0:T(8,128)(2,1)}, bf16[512,1536]{1,0:T(8,128)(2,1)}, u32[]{:S(2)}, u32[]{:S(2)}) collective-permute-start(bf16[512,1536]{1,0:T(8,128)(2,1)} %collective-permute-done.refs_0_), channel_id=1, source_target_pairs={{1,2},{2,3},{5,6},{6,7},{9,10},{10,11},{13,14},{14,15},{17,18},{18... | collective-permute-start | bytes 4718600 | tf_op jit(solution)/shard_map/ppermute | solution.py:138
  58.5 45.2 %copy-start.12 = (f32[512,1]{1,0:T(8,128)}, f32[512,1]{1,0:T(8,128)S(1)}, u32[]{:S(2)}) copy-start(f32[512,1]{1,0:T(8,128)S(1)} %copy.43.refs_2_.refs_3_.refs_4_) | copy-start | bytes 6148
  90.7 35.3 %collective-permute-start.4 = (bf16[512,1536]{1,0:T(8,128)(2,1)S(1)}, bf16[512,1536]{1,0:T(8,128)(2,1)S(1)}, u32[]{:S(2)}, u32[]{:S(2)}) collective-permute-start(bf16[512,1536]{1,0:T(8,128)(2,1)S(1)} %broadcast_select_fusion.refs_0_), channel_id=1, source_target_pairs={{2,3},{1,0},{6,7},{5,4},{10,11},{9,8},{14,15},{13,12},{18,19},{17,... | collective-permute-start | bytes 4718600 | tf_op jit(solution)/shard_map/ppermute | solution.py:157
  103.6 22.4 %copy-start.20 = (f32[6144]{0:T(1024)S(1)}, f32[6144]{0:T(1024)}, u32[]{:S(2)}) copy-start(f32[6144]{0:T(1024)} %param.9) | copy-start | bytes 73732
  136.5 31.6 %copy-start.8 = (bf16[4,288,512]{2,1,0:T(8,128)(2,1)}, bf16[4,288,512]{2,1,0:T(8,128)(2,1)S(1)}, u32[]{:S(2)}) copy-start(bf16[4,288,512]{2,1,0:T(8,128)(2,1)S(1)} %get-tuple-element.15.refs_4_) | copy-start | bytes 3538948
  136.5 31.6 %copy-start.9 = (bf16[288,512]{1,0:T(8,128)(2,1)}, bf16[288,512]{1,0:T(8,128)(2,1)S(1)}, u32[]{:S(2)}) copy-start(bf16[288,512]{1,0:T(8,128)(2,1)S(1)} %get-tuple-element.16.refs_1_) | copy-start | bytes 884740
  136.5 31.6 %copy-start.10 = (bf16[288,512]{1,0:T(8,128)(2,1)}, bf16[288,512]{1,0:T(8,128)(2,1)S(1)}, u32[]{:S(2)}) copy-start(bf16[288,512]{1,0:T(8,128)(2,1)S(1)} %get-tuple-element.17.refs_2_) | copy-start | bytes 884740
  136.5 31.6 %copy-start.11 = (bf16[288,512]{1,0:T(8,128)(2,1)}, bf16[288,512]{1,0:T(8,128)(2,1)S(1)}, u32[]{:S(2)}) copy-start(bf16[288,512]{1,0:T(8,128)(2,1)S(1)} %get-tuple-element.18.refs_3_) | copy-start | bytes 884740
  136.5 37.2 %copy-start.3 = (bf16[288,512]{1,0:T(8,128)(2,1)}, bf16[288,512]{1,0:T(8,128)(2,1)S(1)}, u32[]{:S(2)}) copy-start(bf16[288,512]{1,0:T(8,128)(2,1)S(1)} %get-tuple-element.14.refs_0_) | copy-start | bytes 884740
  136.5 2.9 collective-permute-start.8
  140.4 22.7 %collective-permute-start.12 = (bf16[288,512]{1,0:T(8,128)(2,1)}, bf16[288,512]{1,0:T(8,128)(2,1)S(1)}, u32[]{:S(2)}, u32[]{:S(2)}) collective-permute-start(bf16[288,512]{1,0:T(8,128)(2,1)} %get-tuple-element.27), channel_id=1, source_target_pairs={{0,16},{4,20},{8,24},{12,28},{16,0},{20,4},{24,8},{28,12},{1,17},{... | collective-permute-start | bytes 884744 | tf_op jit(solution)/shard_map/ppermute | solution.py:336
  141.9 22.7 %collective-permute-start.14 = (bf16[288,512]{1,0:T(8,128)(2,1)}, bf16[288,512]{1,0:T(8,128)(2,1)S(1)}, u32[]{:S(2)}, u32[]{:S(2)}) collective-permute-start(bf16[288,512]{1,0:T(8,128)(2,1)} %get-tuple-element.26), channel_id=1, source_target_pairs={{0,24},{4,28},{8,16},{12,20},{16,8},{20,12},{24,0},{28,4},{1,25},{... | collective-permute-start | bytes 884744 | tf_op jit(solution)/shard_map/ppermute | solution.py:336
  143.3 25.4 %collective-permute-start.11 = (bf16[288,512]{1,0:T(8,128)(2,1)S(1)}, bf16[288,512]{1,0:T(8,128)(2,1)}, u32[]{:S(2)}, u32[]{:S(2)}) collective-permute-start(bf16[288,512]{1,0:T(8,128)(2,1)S(1)} %get-tuple-element.17.refs_2_), channel_id=1, source_target_pairs={{0,16},{4,20},{8,24},{12,28},{16,0},{20,4},{24,8},{28,12},{1,17},{... | collective-permute-start | bytes 884744 | tf_op jit(solution)/shard_map/ppermute | solution.py:336
  144.8 28.5 %collective-permute-start.13 = (bf16[288,512]{1,0:T(8,128)(2,1)S(1)}, bf16[288,512]{1,0:T(8,128)(2,1)}, u32[]{:S(2)}, u32[]{:S(2)}) collective-permute-start(bf16[288,512]{1,0:T(8,128)(2,1)S(1)} %get-tuple-element.18.refs_3_), channel_id=1, source_target_pairs={{0,24},{4,28},{8,16},{12,20},{16,8},{20,12},{24,0},{28,4},{1,25},{... | collective-permute-start | bytes 884744 | tf_op jit(solution)/shard_map/ppermute | solution.py:336
  145.9 27.8 %collective-permute-start.9 = (bf16[288,512]{1,0:T(8,128)(2,1)S(1)}, bf16[288,512]{1,0:T(8,128)(2,1)}, u32[]{:S(2)}, u32[]{:S(2)}) collective-permute-start(bf16[288,512]{1,0:T(8,128)(2,1)S(1)} %get-tuple-element.16.refs_1_), channel_id=1, source_target_pairs={{0,8},{4,12},{8,0},{12,4},{16,24},{20,28},{24,16},{28,20},{1,9},{5... | collective-permute-start | bytes 884744 | tf_op jit(solution)/shard_map/ppermute | solution.py:336
  163.1 10.7 %copy-start.17 = (s32[54]{0:T(128)S(1)}, s32[54]{0:T(128)}, u32[]{:S(2)}) copy-start(s32[54]{0:T(128)} %copy-done.15) | copy-start | bytes 652
  163.1 10.7 %copy-start.18 = (s32[8,8]{1,0:T(8,128)S(1)}, s32[8,8]{1,0:T(8,128)}, u32[]{:S(2)}) copy-start(s32[8,8]{1,0:T(8,128)} %pair_ref.1) | copy-start | bytes 772
  163.1 10.7 %collective-permute-start.10 = (bf16[288,512]{1,0:T(8,128)(2,1)}, bf16[288,512]{1,0:T(8,128)(2,1)}, u32[]{:S(2)}, u32[]{:S(2)}) collective-permute-start(bf16[288,512]{1,0:T(8,128)(2,1)} %get-tuple-element.28), channel_id=1, source_target_pairs={{0,8},{4,12},{8,0},{12,4},{16,24},{20,28},{24,16},{28,20},{1,9},{5... | collective-permute-start | bytes 884744 | tf_op jit(solution)/shard_map/ppermute | solution.py:336
  168.1 26.0 %collective-permute-start.24 = (bf16[96,1536]{1,0:T(8,128)(2,1)}, bf16[96,1536]{1,0:T(8,128)(2,1)S(1)}, u32[]{:S(2)}, u32[]{:S(2)}) collective-permute-start(bf16[96,1536]{1,0:T(8,128)(2,1)} %get-tuple-element.23), channel_id=1, source_target_pairs={{0,1},{1,2},{2,3},{3,0},{4,5},{5,6},{6,7},{7,4},{8,9},{9,10},{10,1... | collective-permute-start | bytes 884744 | tf_op jit(solution)/shard_map/ppermute | solution.py:134
  168.7 25.4 %collective-permute-start.25 = (bf16[96,1536]{1,0:T(8,128)(2,1)}, bf16[96,1536]{1,0:T(8,128)(2,1)S(1)}, u32[]{:S(2)}, u32[]{:S(2)}) collective-permute-start(bf16[96,1536]{1,0:T(8,128)(2,1)} %get-tuple-element.24), channel_id=1, source_target_pairs={{0,2},{1,3},{2,0},{3,1},{4,6},{5,7},{6,4},{7,5},{8,10},{9,11},{10,... | collective-permute-start | bytes 884744 | tf_op jit(solution)/shard_map/ppermute | solution.py:134
  173.3 20.9 %collective-permute-start.26 = (bf16[96,1536]{1,0:T(8,128)(2,1)}, bf16[96,1536]{1,0:T(8,128)(2,1)S(1)}, u32[]{:S(2)}, u32[]{:S(2)}) collective-permute-start(bf16[96,1536]{1,0:T(8,128)(2,1)} %get-tuple-element.25), channel_id=1, source_target_pairs={{0,3},{1,0},{2,1},{3,2},{4,7},{5,4},{6,5},{7,6},{8,11},{9,8},{10,9... | collective-permute-start | bytes 884744 | tf_op jit(solution)/shard_map/ppermute | solution.py:134
  194.1 6.6 %copy-start.2 = (bf16[2,96,512]{2,1,0:T(8,128)(2,1)S(1)}, bf16[2,96,512]{2,1,0:T(8,128)(2,1)}, u32[]{:S(2)}) copy-start(bf16[2,96,512]{2,1,0:T(8,128)(2,1)} %copy-done.1) | copy-start | bytes 589828
  197.2 8.7 %collective-permute-start.17 = (bf16[2,96,512]{2,1,0:T(8,128)(2,1)S(1)}, bf16[2,96,512]{2,1,0:T(8,128)(2,1)S(1)}, u32[]{:S(2)}, u32[]{:S(2)}) collective-permute-start(bf16[2,96,512]{2,1,0:T(8,128)(2,1)S(1)} %get-tuple-element.22), channel_id=1, source_target_pairs={{0,24},{4,28},{8,16},{12,20},{16,8},{20,12},{24,0},{28,4},{1,25},{... | collective-permute-start | bytes 589832 | tf_op jit(solution)/shard_map/ppermute | solution.py:336
  199.2 8.8 %collective-permute-start.16 = (bf16[2,96,512]{2,1,0:T(8,128)(2,1)S(1)}, bf16[2,96,512]{2,1,0:T(8,128)(2,1)S(1)}, u32[]{:S(2)}, u32[]{:S(2)}) collective-permute-start(bf16[2,96,512]{2,1,0:T(8,128)(2,1)S(1)} %get-tuple-element.21), channel_id=1, source_target_pairs={{0,16},{4,20},{8,24},{12,28},{16,0},{20,4},{24,8},{28,12},{1,17},{... | collective-permute-start | bytes 589832 | tf_op jit(solution)/shard_map/ppermute | solution.py:336
  199.7 8.3 %collective-permute-start.15 = (bf16[2,96,512]{2,1,0:T(8,128)(2,1)S(1)}, bf16[2,96,512]{2,1,0:T(8,128)(2,1)S(1)}, u32[]{:S(2)}, u32[]{:S(2)}) collective-permute-start(bf16[2,96,512]{2,1,0:T(8,128)(2,1)S(1)} %get-tuple-element.20), channel_id=1, source_target_pairs={{0,8},{4,12},{8,0},{12,4},{16,24},{20,28},{24,16},{28,20},{1,9},{5... | collective-permute-start | bytes 589832 | tf_op jit(solution)/shard_map/ppermute | solution.py:336
  208.1 1.8 collective-permute-start.18
  213.0 27.8 %collective-permute-start.19 = (bf16[768,512]{1,0:T(8,128)(2,1)}, bf16[768,512]{1,0:T(8,128)(2,1)S(1)}, u32[]{:S(2)}, u32[]{:S(2)}) collective-permute-start(bf16[768,512]{1,0:T(8,128)(2,1)} %bitcast.60), channel_id=1, source_target_pairs={{0,1},{1,2},{2,3},{4,5},{5,6},{6,7},{8,9},{9,10},{10,11},{12,13},{... | collective-permute-start | bytes 2359304 | tf_op jit(solution)/shard_map/ppermute | solution.py:138
  223.4 21.4 %collective-permute-start.21 = (bf16[768,512]{1,0:T(8,128)(2,1)}, bf16[768,512]{1,0:T(8,128)(2,1)S(1)}, u32[]{:S(2)}, u32[]{:S(2)}) collective-permute-start(bf16[768,512]{1,0:T(8,128)(2,1)} %bitcast.61), channel_id=1, source_target_pairs={{3,2},{2,1},{1,0},{7,6},{6,5},{5,4},{11,10},{10,9},{9,8},{15,14},{... | collective-permute-start | bytes 2359304 | tf_op jit(solution)/shard_map/ppermute | solution.py:138
  240.8 5.4 %copy-start.34 = (bf16[768,512]{1,0:T(8,128)(2,1)}, bf16[768,512]{1,0:T(8,128)(2,1)S(1)}, u32[]{:S(2)}) copy-start(bf16[768,512]{1,0:T(8,128)(2,1)S(1)} %collective-permute-done.19.refs_1_) | copy-start | bytes 2359300
  240.8 5.3 %collective-permute-start.20 = (bf16[768,512]{1,0:T(8,128)(2,1)S(1)}, bf16[768,512]{1,0:T(8,128)(2,1)S(1)}, u32[]{:S(2)}, u32[]{:S(2)}) collective-permute-start(bf16[768,512]{1,0:T(8,128)(2,1)S(1)} %collective-permute-done.19.refs_1_), channel_id=1, source_target_pairs={{1,2},{2,3},{5,6},{6,7},{9,10},{10,11},{13,14},{14,15},{17,18},{18... | collective-permute-start | bytes 2359304 | tf_op jit(solution)/shard_map/ppermute | solution.py:138
  244.8 20.4 %copy-start.35 = (bf16[768,512]{1,0:T(8,128)(2,1)}, bf16[768,512]{1,0:T(8,128)(2,1)S(1)}, u32[]{:S(2)}) copy-start(bf16[768,512]{1,0:T(8,128)(2,1)S(1)} %collective-permute-done.21.refs_2_.refs_3_) | copy-start | bytes 2359300
  244.8 20.4 %collective-permute-start.22 = (bf16[768,512]{1,0:T(8,128)(2,1)S(1)}, bf16[768,512]{1,0:T(8,128)(2,1)S(1)}, u32[]{:S(2)}, u32[]{:S(2)}) collective-permute-start(bf16[768,512]{1,0:T(8,128)(2,1)S(1)} %collective-permute-done.21.refs_2_.refs_3_), channel_id=1, source_target_pairs={{2,1},{1,0},{6,5},{5,4},{10,9},{9,8},{14,13},{13,12},{18,17},{17,1... | collective-permute-start | bytes 2359304 | tf_op jit(solution)/shard_map/ppermute | solution.py:138
  246.2 24.0 %copy-start.22 = (bf16[768,512]{1,0:T(8,128)(2,1)}, bf16[768,512]{1,0:T(8,128)(2,1)S(1)}, u32[]{:S(2)}) copy-start(bf16[768,512]{1,0:T(8,128)(2,1)S(1)} %collective-permute-done.20.refs_5_) | copy-start | bytes 2359300
  265.3 4.9 %copy-start.23 = (bf16[768,512]{1,0:T(8,128)(2,1)}, bf16[768,512]{1,0:T(8,128)(2,1)S(1)}, u32[]{:S(2)}) copy-start(bf16[768,512]{1,0:T(8,128)(2,1)S(1)} %collective-permute-done.22.refs_4_) | copy-start | bytes 2359300
  265.4 4.8 %copy-start.21 = (bf16[768,512]{1,0:T(8,128)(2,1)}, bf16[768,512]{1,0:T(8,128)(2,1)S(1)}, u32[]{:S(2)}) copy-start(bf16[768,512]{1,0:T(8,128)(2,1)S(1)} %broadcast_select_fusion.1.refs_0_) | copy-start | bytes 2359300
  265.4 19.8 %collective-permute-start.23 = (bf16[768,512]{1,0:T(8,128)(2,1)S(1)}, bf16[768,512]{1,0:T(8,128)(2,1)S(1)}, u32[]{:S(2)}, u32[]{:S(2)}) collective-permute-start(bf16[768,512]{1,0:T(8,128)(2,1)S(1)} %broadcast_select_fusion.1.refs_0_), channel_id=1, source_target_pairs={{2,3},{1,0},{6,7},{5,4},{10,11},{9,8},{14,15},{13,12},{18,19},{17,... | collective-permute-start | bytes 2359304 | tf_op jit(solution)/shard_map/ppermute | solution.py:157
  (17 other events, 21.0 us)
Sparse Core Ops, SparseCore 0:
  197.3 50.4 all-gather.2
where the time goes:
time: 299 us; the launch traced here: 298 us
  waiting for transfers between devices  127 us (42%)
  Pallas kernels  86 us (29%)
  starting transfers between devices  50.7 us (17%)
  local copies, waits for them, and re-layouts  14.9 us (5%)
  between operations  14.8 us (5%)
  other arithmetic  4.74 us (2%)
    ppermute x8, waiting for transfers between devices, line_hop(): return (lax.ppermute(up, 'tp', ups), lax.ppermute(down, 'tp', downs))  88.2 us
    pallas_call x4, Pallas kernels, project(): pl.pallas_call(functools.partial(project_kernel, step, len(shards)), grid...  40.8 us
    ppermute x11, waiting for transfers between devices, swap(): lax.ppermute(value, 'blk', [(place, place ^ distance) for place in range(...  27.9 us
    ppermute x8, starting transfers between devices, line_hop(): return (lax.ppermute(up, 'tp', ups), lax.ppermute(down, 'tp', downs))  23.9 us
    pallas_call x1, Pallas kernels, attend(): pl.pallas_call(attend_kernel, in_specs=[smem, smem, vmem] + [vmem] * len(...  17.7 us
    pallas_call x2, Pallas kernels, combine(): pl.pallas_call(functools.partial(combine_kernel, steps, tuple((len(step)...  16.9 us
    ppermute x6, starting transfers between devices, turn(): lax.ppermute(value, 'tp', [(source, (source + distance) % 4) for source i...  12.1 us
    ppermute x11, starting transfers between devices, swap(): lax.ppermute(value, 'blk', [(place, place ^ distance) for place in range(...  11.6 us
  transfers between devices with their start and end apart: 28, of which 12 were waited for; matrix products, arithmetic and copies ran while one was open for 3% of the time, Pallas kernels for 23%

commit v1 on v0

--- a/solution.py
+++ b/solution.py
@@ -13,6 +13,7 @@
 
 
 EPSILON = 1e-05
+QUERY_SCALE = HD ** (-0.5) * 1.4426950408889634
 
 
 def from_behind(value, axis, steps):
@@ -185,9 +186,9 @@
         refs[0][0] = total
         return
     cos_ref, sin_ref = refs[:2]
-    kept_refs, given_ref = refs[2:6], refs[6]
+    kept_refs, given_ref = refs[5:9], refs[9]
     chip, core = facts_ref[CHIP], facts_ref[CORE]
-    turned = total.T
+    turned = total.T * jnp.where(kind == 0, QUERY_SCALE, 1.0)
     turned_ref[...] = turned.reshape(turned_ref.shape).astype(jnp.bfloat16)
 
     @pl.when(kind < 2)
@@ -204,7 +205,7 @@
         given_ref[distance] = turned_ref[head + 1 - core]
 
 
-def project(step, facts, shards, mean, rstd, gain, w3, previous, tables):
+def project(step, facts, shards, mean, rstd, gain, w3, previous, tables, waited):
     rows, depth = shards[0].shape
     width = w3.shape[2]
     column = pl.BlockSpec((rows, 1), lambda c, o: (0, 0))
@@ -222,7 +223,8 @@
     out_shape, out_specs = jax.ShapeDtypeStruct((3, rows, width), jnp.float32), sums
     if step == 3:
         in_specs += [pl.BlockSpec((ROT, rows), lambda c, o: (0, 0))] * 2
-        args += tables
+        in_specs += [pl.BlockSpec(memory_space=pl.ANY)] * len(waited)
+        args += tables + waited
         out_shape = [jax.ShapeDtypeStruct((3 * HD, rows), jnp.bfloat16)] * 4
         out_shape.append(jax.ShapeDtypeStruct((4, 3 * HD, rows), jnp.bfloat16))
         out_specs = [pl.BlockSpec((HD, rows), lambda c, o: (c, 0))] * 4
@@ -242,7 +244,7 @@
         out_shape=out_shape,
         compiler_params=pltpu.CompilerParams(vmem_limit_bytes=48 << 20),
         cost_estimate=pl.CostEstimate(
-            flops=24 * rows * depth * width, bytes_accessed=6 * depth * width, transcendentals=0
+            flops=(1, 20, 20, 6)[step] * rows * depth * width, bytes_accessed=0, transcendentals=0
         ),
         name="project",
     )(facts, *args)
@@ -258,8 +260,6 @@
             q_ref[block] = piece[:HD]
             k_ref[block] = piece[HD : 2 * HD].T
             v_ref[block] = piece[2 * HD :]
-    scale = HD ** (-0.5) * 1.4426950408889634
-
     def one_block(block, carry):
         token = block * rows + lax.broadcasted_iota(jnp.int32, (1, rows), 1)
         start = start_ref[block]
@@ -268,7 +268,7 @@
         acc_ref[...] = jnp.zeros_like(acc_ref)
 
         def update(other, masked):
-            scores = jnp.dot(k_ref[other], q_ref[block], preferred_element_type=jnp.float32) * scale
+            scores = jnp.dot(k_ref[other], q_ref[block], preferred_element_type=jnp.float32)
             if masked:
                 key = other * rows + lax.broadcasted_iota(jnp.int32, (rows, rows), 0)
                 scores = jnp.where((key >= start) & (key <= token), scores, -jnp.inf)
@@ -355,7 +355,7 @@
 
 def to_blocks(facts, mixed):
     core = lax.axis_index("blk") % 2
-    held = [pair if distance == 0 else swap(pair, 2 * distance) for distance, pair in enumerate(mixed)]
+    held = mixed[:1] + [swap(mixed[distance], 2 * distance) for distance in (1, 2, 3)]
     given = [lax.dynamic_index_in_dim(pair, 1 - core, 0, keepdims=False) for pair in held]
     got = swap(jnp.stack(given), 1)
     vmem = pl.BlockSpec(memory_space=pltpu.VMEM)
@@ -410,7 +410,9 @@
     in_specs = [pl.BlockSpec((depth, rows), lambda n, k, o: (0, 0)) for step in arrays for _ in step]
     args = [array for step in arrays for array in step]
     if 0 in steps:
-        in_specs.append(pl.BlockSpec((1, 1, depth, tile), lambda n, k, o: (0, 0, 0, n)))
+        in_specs.append(
+            pl.BlockSpec((depth, tile), lambda n, k, o: (0, o[OWNER] * (width // tile) + n))
+        )
         args.append(own)
     in_specs.append(
         pl.BlockSpec((outer, 1, inner, tile), lambda n, k, o: (0, o[COLUMN + steps[0] + k], 0, n))
@@ -440,7 +442,7 @@
 
 
 def share_kernel(facts_ref, w_ref, *refs):
-    outs, sems = refs[-4:-1], refs[-1]
+    outs, sems = refs[:3], refs[3]
     rows, width = outs[0].shape
     first = facts_ref[0] * rows
     copies = []
@@ -454,17 +456,17 @@
         copy.wait()
 
 
-def shares(numbers, w_out, width, waited):
+def shares(numbers, w_out, width):
     any_space = pl.BlockSpec(memory_space=pl.ANY)
     return pl.pallas_call(
         share_kernel,
-        in_specs=[pl.BlockSpec(memory_space=pltpu.SMEM), any_space] + [any_space] * len(waited),
+        in_specs=[pl.BlockSpec(memory_space=pltpu.SMEM), any_space],
         out_specs=[pl.BlockSpec(memory_space=pltpu.VMEM)] * 3,
         out_shape=[jax.ShapeDtypeStruct((HD, width), w_out.dtype)] * 3,
         scratch_shapes=[pltpu.SemaphoreType.DMA((3,))],
         cost_estimate=pl.CostEstimate(flops=0, bytes_accessed=2 << 20, transcendentals=0),
         name="shares",
-    )(numbers, w_out, *waited)
+    )(numbers, w_out)
 
 
 def stack_kernel(*refs):
@@ -559,11 +561,14 @@
         ]
     )
 
+    windows = jnp.stack([block] + [(place + distance) % 4 for distance in (1, 2, 3)]).astype(jnp.int32)
+    windows = shares(windows, w_out, depth)
+    windows = list(windows)
     total = [None]
 
     def take_in(step, arrays):
         total[0] = project(
-            step, facts, arrays, mean, rstd, gain, w3, total[0], [cosine, sine]
+            step, facts, arrays, mean, rstd, gain, w3, total[0], [cosine, sine], windows
         )
 
     gather_line(hidden_in, take_in)
@@ -571,22 +576,19 @@
     arrived = to_heads(kept, swap(given, 1))
     page_cache = pages(facts, page_count, [*kept, given])
 
-    windows = jnp.stack([block] + [(place + distance) % 4 for distance in (1, 2, 3)]).astype(jnp.int32)
-    windows = shares(windows, w_out, depth, [arrived[5], arrived[7]])
     columns = [turn(window, distance) for distance, window in zip((1, 2, 3), windows)]
-    mixed = attend(facts, pair_table, start, arrived)
+    mixed = list(attend(facts, pair_table, start, arrived))
     others = lax.all_gather(stack(columns, mixed[:1]), "blk", axis=0)
     heads = to_blocks(facts, mixed)
-    own = lax.dynamic_slice_in_dim(w_out, place * depth, depth, 1).reshape(1, 1, width, depth)
 
     came, result = [], [None]
 
     def add_in(step, arrays):
         came.append(arrays)
         if step == 2:
-            result[0] = combine((0, 1, 2), facts, came[:3], own, others)
+            result[0] = combine((0, 1, 2), facts, came[:3], w_out, others)
         if step == 3:
-            result[0] = combine((3,), facts, came[3:], own, others, result[0])
+            result[0] = combine((3,), facts, came[3:], None, others, result[0])
 
     gather_line(heads, add_in)
     attn_out = result[0]

time: 299 us -> 283 us (0.946)
  local copies, waits for them, and re-layouts: 14.9 us -> 5.96 us
  waiting for transfers between devices: 127 us -> 120 us
    ppermute x11, waiting for transfers between devices: 27.9 us -> 20.4 us  [swap(): lax.ppermute(value, 'blk', [(place, place ^ distance) for place in range(...]
    ppermute x8, starting transfers between devices: 23.9 us -> 17.8 us  [line_hop(): return (lax.ppermute(up, 'tp', ups), lax.ppermute(down, 'tp', downs))]
    ppermute x2, waiting for transfers between devices: 10.9 us -> 15.9 us  [gather_line(): outer = lax.ppermute(inner, 'tp', [(2, 3), (1, 0)])]
    ppermute x8, waiting for transfers between devices: 88.2 us -> 84 us  [line_hop(): return (lax.ppermute(up, 'tp', ups), lax.ppermute(down, 'tp', downs))]
    ppermute x6, starting transfers between devices: 12.1 us -> 16.4 us  [turn(): lax.ppermute(value, 'tp', [(source, (source + distance) % 4) for source i...]
    unnamed x74 -> x62, local copies, waits for them, and re-layouts: 8.42 us -> 5.04 us
    reshape x1 -> x0, local copies, waits for them, and re-layouts: 3.29 us -> none  [per_device_heads(): lax.dynamic_slice_in_dim(w_out, place * depth, depth, 1)]
  transfers between devices with their start and end apart: 28 -> 28, of which waited for: 12 -> 12; matrix products, arithmetic and copies ran while one was open for 3% -> 2% of each run, Pallas kernels for 23% -> 24%
where the time goes in v1:
time: 283 us; the launch traced here: 282 us
  waiting for transfers between devices  120 us (42%)
  Pallas kernels  85.1 us (30%)
  starting transfers between devices  50 us (18%)
  between operations  14.8 us (5%)
  local copies, waits for them, and re-layouts  5.96 us (2%)
  other arithmetic  5.38 us (2%)
    ppermute x8, waiting for transfers between devices, line_hop(): return (lax.ppermute(up, 'tp', ups), lax.ppermute(down, 'tp', downs))  84 us
    pallas_call x4, Pallas kernels, project(): pl.pallas_call(functools.partial(project_kernel, step, len(shards)), grid...  41.7 us
    ppermute x11, waiting for transfers between devices, swap(): lax.ppermute(value, 'blk', [(place, place ^ distance) for place in range(...  20.4 us
    ppermute x8, starting transfers between devices, line_hop(): return (lax.ppermute(up, 'tp', ups), lax.ppermute(down, 'tp', downs))  17.8 us
    pallas_call x2, Pallas kernels, combine(): pl.pallas_call(functools.partial(combine_kernel, steps, tuple((len(step)...  16.9 us
    ppermute x6, starting transfers between devices, turn(): lax.ppermute(value, 'tp', [(source, (source + distance) % 4) for source i...  16.4 us
    ppermute x2, waiting for transfers between devices, gather_line(): outer = lax.ppermute(inner, 'tp', [(2, 3), (1, 0)])  15.9 us
    pallas_call x1, Pallas kernels, attend(): pl.pallas_call(attend_kernel, in_specs=[smem, smem, vmem] + [vmem] * len(...  15.8 us
  transfers between devices with their start and end apart: 28, of which 12 were waited for; matrix products, arithmetic and copies ran while one was open for 2% of the time, Pallas kernels for 24%

profile of v1, /device:TPU:0, one launch (start us, length us, event | category | flops | bytes accessed | tf_op | source)
XLA Modules:
  0.0 281.5 jit_solution(15919470023952986903)
XLA Ops:
  7.2 1.4 collective-permute-start.2
  8.7 6.8 %collective-permute-start = (bf16[512,1536]{1,0:T(8,128)(2,1)}, bf16[512,1536]{1,0:T(8,128)(2,1)}, u32[]{:S(2)}, u32[]{:S(2)}) collective-permute-start(bf16[512,1536]{1,0:T(8,128)(2,1)} %refs_0_.1), channel_id=1, source_target_pairs={{0,1},{1,2},{2,3},{4,5},{5,6},{6,7},{8,9},{9,10},{10,11},{12,13},{... | collective-permute-start | bytes 4718600 | tf_op jit(solution)/shard_map/ppermute | solution.py:139
  15.5 1.7 convert_reduce_fusion
  17.7 0.9 collective-permute-start.5
  18.6 2.2 collective-permute-start.6
  20.8 2.8 %collective-permute-start.7 = (f32[2,512]{1,0:T(2,128)S(1)}, f32[2,512]{1,0:T(2,128)S(1)}, u32[]{:S(2)}, u32[]{:S(2)}) collective-permute-start(f32[2,512]{1,0:T(2,128)S(1)} %get-tuple-element.31), channel_id=1, source_target_pairs={{0,3},{1,0},{2,1},{3,2},{4,7},{5,4},{6,5},{7,6},{8,11},{9,8},{10,9... | collective-permute-start | bytes 12296 | tf_op jit(solution)/shard_map/ppermute | solution.py:135
  24.3 22.8 %collective-permute-done.2.refs_1_.refs_0_ = bf16[512,1536]{1,0:T(8,128)(2,1)} collective-permute-done((bf16[512,1536]{1,0:T(8,128)(2,1)}, bf16[512,1536]{1,0:T(8,128)(2,1)}, u32[]{:S(2)}, u32[]{:S(2)}) %collective-permute-start.2) | collective-permute-done | bytes 1572896 | tf_op jit(solution)/shard_map/ppermute | solution.py:139
  47.1 1.3 collective-permute-start.3
  48.4 1.8 collective-permute-start.1
  51.5 2.9 %shares.1 = (bf16[96,1536]{1,0:T(8,128)(2,1)}, bf16[96,1536]{1,0:T(8,128)(2,1)}, bf16[96,1536]{1,0:T(8,128)(2,1)}) custom-call(s32[4]{0:T(128)} %pad_add_fusion.facts_ref, bf16[768,6144]{1,0:T(8,128)(2,1)} %refs_6_.1), custom_call_target="tpu_custom_call" | custom-call | bytes 2097152 | tf_op jit(solution)/shard_map/shares/pallas_call | solution.py:461
  55.0 9.0 %project.4.refs_6_ = f32[3,512,768]{2,1,0:T(8,128)} custom-call(s32[54]{0:T(128)S(1)} %concatenate.9.facts_ref, bf16[512,1536]{1,0:T(8,128)(2,1)S(1)} %copy-done, f32[512,1]{1,0:T(8,128)S(1)} %copy.42.refs_1_.refs_2_.refs_3_, f32[512,1]{1,0:T(8,128)S(1)} %copy.43.refs_2_.refs_3_.refs_4_, f32[4,1,1536]{2,1,0:T(1,128)S(1)} %bitcast.50, ...), custom_call_target="tpu_custom_call" | custom-call | flops 603979776 | tf_op jit(solution)/shard_map/project/pallas_call | solution.py:232
  64.1 20.7 %collective-permute-done.3.refs_1_ = bf16[512,1536]{1,0:T(8,128)(2,1)} collective-permute-done((bf16[512,1536]{1,0:T(8,128)(2,1)}, bf16[512,1536]{1,0:T(8,128)(2,1)}, u32[]{:S(2)}, u32[]{:S(2)}) %collective-permute-start.3) | collective-permute-done | bytes 1572896 | tf_op jit(solution)/shard_map/ppermute | solution.py:139
  84.8 1.6 broadcast_select_fusion.refs_0_
  86.4 1.5 collective-permute-start.4
  87.9 11.4 %project.5.refs_7_ = f32[3,512,768]{2,1,0:T(8,128)} custom-call(s32[54]{0:T(128)S(1)} %concatenate.9.facts_ref, bf16[512,1536]{1,0:T(8,128)(2,1)} %collective-permute-done.refs_0_, bf16[512,1536]{1,0:T(8,128)(2,1)} %collective-permute-done.2.refs_1_.refs_0_, f32[512,1]{1,0:T(8,128)S(1)} %copy.42.refs_1_.refs_2_.refs_3_, ...), custom_call_target="tpu_custom_call" | custom-call | flops 12079595520 | tf_op jit(solution)/shard_map/project/pallas_call | solution.py:232
  99.3 11.9 %project.6.refs_6_ = f32[3,512,768]{2,1,0:T(8,128)} custom-call(s32[54]{0:T(128)S(1)} %concatenate.9.facts_ref, bf16[512,1536]{1,0:T(8,128)(2,1)} %collective-permute-done.2.refs_1_.refs_0_, bf16[512,1536]{1,0:T(8,128)(2,1)} %collective-permute-done.3.refs_1_, bf16[512,1536]{1,0:T(8,128)(2,1)} %collective-permute-done.1.refs_2_, ...), custom_call_target="tpu_custom_call" | custom-call | flops 12079595520 | tf_op jit(solution)/shard_map/project/pallas_call | solution.py:232
  111.2 12.3 %collective-permute-done.4.refs_1_ = bf16[512,1536]{1,0:T(8,128)(2,1)S(1)} collective-permute-done((bf16[512,1536]{1,0:T(8,128)(2,1)S(1)}, bf16[512,1536]{1,0:T(8,128)(2,1)S(1)}, u32[]{:S(2)}, u32[]{:S(2)}) %collective-permute-start.4) | collective-permute-done | bytes 1572896 | tf_op jit(solution)/shard_map/ppermute | solution.py:158
  123.5 1.1 copy-done.15
  124.7 9.3 %project.7 = (bf16[288,512]{1,0:T(8,128)(2,1)S(1)}, bf16[288,512]{1,0:T(8,128)(2,1)S(1)}, bf16[288,512]{1,0:T(8,128)(2,1)S(1)}, bf16[288,512]{1,0:T(8,128)(2,1)S(1)}, bf16[4,288,512]{2,1,0:T(8,128)(2,1)S(1)}) custom-call(s32[54]{0:T(128)S(1)} %concatenate.9.facts_ref, bf16[512,1536]{1,0:T(8,128)(2,1)S(1)} %broadcast_select_fusion.refs_0_, ...), custom_call_target="tpu_custom_call" | custom-call | flops 3623878656 | tf_op jit(solution)/shard_map/project/pallas_call | solution.py:232
  134.2 1.6 collective-permute-start.11
  135.8 1.4 collective-permute-start.13
  137.8 1.6 collective-permute-start.10
  139.4 1.5 collective-permute-start.12
  140.9 9.5 %collective-permute-done.11.refs_4_ = bf16[288,512]{1,0:T(8,128)(2,1)S(1)} collective-permute-done((bf16[288,512]{1,0:T(8,128)(2,1)S(1)}, bf16[288,512]{1,0:T(8,128)(2,1)S(1)}, u32[]{:S(2)}, u32[]{:S(2)}) %collective-permute-start.11) | collective-permute-done | bytes 294944 | tf_op jit(solution)/shard_map/ppermute | solution.py:336
  150.4 2.4 collective-permute-start.14
  152.8 5.6 %collective-permute-start.25 = (bf16[96,1536]{1,0:T(8,128)(2,1)S(1)}, bf16[96,1536]{1,0:T(8,128)(2,1)S(1)}, u32[]{:S(2)}, u32[]{:S(2)}) collective-permute-start(bf16[96,1536]{1,0:T(8,128)(2,1)S(1)} %copy-done.9), channel_id=1, source_target_pairs={{0,2},{1,3},{2,0},{3,1},{4,6},{5,7},{6,4},{7,5},{8,10},{9,11},{10,... | collective-permute-start | bytes 884744 | tf_op jit(solution)/shard_map/ppermute | solution.py:135
  158.4 4.9 %collective-permute-start.26 = (bf16[96,1536]{1,0:T(8,128)(2,1)S(1)}, bf16[96,1536]{1,0:T(8,128)(2,1)S(1)}, u32[]{:S(2)}, u32[]{:S(2)}) collective-permute-start(bf16[96,1536]{1,0:T(8,128)(2,1)S(1)} %copy-done.8), channel_id=1, source_target_pairs={{0,3},{1,0},{2,1},{3,2},{4,7},{5,4},{6,5},{7,6},{8,11},{9,8},{10,9... | collective-permute-start | bytes 884744 | tf_op jit(solution)/shard_map/ppermute | solution.py:135
  163.3 1.5 collective-permute-done.14.refs_7_
  164.8 15.8 %attend.1 = (bf16[2,96,512]{2,1,0:T(8,128)(2,1)S(1)}, bf16[2,96,512]{2,1,0:T(8,128)(2,1)S(1)}, bf16[2,96,512]{2,1,0:T(8,128)(2,1)S(1)}, bf16[2,96,512]{2,1,0:T(8,128)(2,1)S(1)}) custom-call(s32[54]{0:T(128)S(1)} %concatenate.9.facts_ref, s32[8,8]{1,0:T(8,128)S(1)} %copy-done.13, s32[8,1,512]{2,1,0:T(1,128)S(1)} %bitcast.55, ...), custom_call_target="tpu_custom_call" | custom-call | flops 1000 | bytes 1000 | tf_op jit(solution)/shard_map/attend/pallas_call | solution.py:315
  182.9 2.2 stack.114
  185.0 1.5 collective-permute-start.17
  186.6 1.5 collective-permute-start.16
  188.6 5.3 %collective-permute-done.17.refs_3_ = bf16[2,96,512]{2,1,0:T(8,128)(2,1)S(1)} collective-permute-done((bf16[2,96,512]{2,1,0:T(8,128)(2,1)S(1)}, bf16[2,96,512]{2,1,0:T(8,128)(2,1)S(1)}, u32[]{:S(2)}, u32[]{:S(2)}) %collective-permute-start.17) | collective-permute-done | bytes 196640 | tf_op jit(solution)/shard_map/ppermute | solution.py:336
  193.9 2.5 collective-permute-done.16.refs_2_
  196.6 1.7 collective-permute-done.18.refs_4_
  199.0 2.3 order.1
  201.3 3.2 %collective-permute-start.19 = (bf16[768,512]{1,0:T(8,128)(2,1)}, bf16[768,512]{1,0:T(8,128)(2,1)S(1)}, u32[]{:S(2)}, u32[]{:S(2)}) collective-permute-start(bf16[768,512]{1,0:T(8,128)(2,1)} %bitcast.62), channel_id=1, source_target_pairs={{0,1},{1,2},{2,3},{4,5},{5,6},{6,7},{8,9},{9,10},{10,11},{12,13},{... | collective-permute-start | bytes 2359304 | tf_op jit(solution)/shard_map/ppermute | solution.py:139
  204.6 1.3 collective-permute-start.21
  205.9 16.0 %collective-permute-done.19.refs_1_ = bf16[768,512]{1,0:T(8,128)(2,1)S(1)} collective-permute-done((bf16[768,512]{1,0:T(8,128)(2,1)}, bf16[768,512]{1,0:T(8,128)(2,1)S(1)}, u32[]{:S(2)}, u32[]{:S(2)}) %collective-permute-start.19) | collective-permute-done | bytes 786464 | tf_op jit(solution)/shard_map/ppermute | solution.py:139
  222.6 3.9 %collective-permute-done.21.refs_2_.refs_3_ = bf16[768,512]{1,0:T(8,128)(2,1)S(1)} collective-permute-done((bf16[768,512]{1,0:T(8,128)(2,1)}, bf16[768,512]{1,0:T(8,128)(2,1)S(1)}, u32[]{:S(2)}, u32[]{:S(2)}) %collective-permute-start.21) | collective-permute-done | bytes 786464 | tf_op jit(solution)/shard_map/ppermute | solution.py:139
  226.6 1.3 collective-permute-start.22
  227.9 20.4 %collective-permute-done.22.refs_4_ = bf16[768,512]{1,0:T(8,128)(2,1)S(1)} collective-permute-done((bf16[768,512]{1,0:T(8,128)(2,1)S(1)}, bf16[768,512]{1,0:T(8,128)(2,1)S(1)}, u32[]{:S(2)}, u32[]{:S(2)}) %collective-permute-start.22) | collective-permute-done | bytes 786464 | tf_op jit(solution)/shard_map/ppermute | solution.py:139
  248.4 1.5 collective-permute-start.23
  249.9 3.3 %pages.1 = bf16[2,32,16,768]{3,2,1,0:T(8,128)(2,1)} custom-call(s32[54]{0:T(128)} %copy-done.12, bf16[288,512]{1,0:T(8,128)(2,1)} %copy-done.3, bf16[288,512]{1,0:T(8,128)(2,1)} %copy-done.5, bf16[288,512]{1,0:T(8,128)(2,1)} %copy-done.6, bf16[288,512]{1,0:T(8,128)(2,1)} %copy-done.7, bf16[4,288,512]{2,1,0:T(8,128)(2,1)} %copy-done.4), custom_call_target="tpu_custom_call" | custom-call | bytes 10485760 | tf_op jit(solution)/shard_map/pages/pallas_call | solution.py:510
  253.3 11.7 %combine.2.refs_3_ = bf16[512,1536]{1,0:T(8,128)(2,1)} custom-call(s32[54]{0:T(128)} %copy-done.12, bf16[768,512]{1,0:T(8,128)(2,1)} %bitcast.64, bf16[768,512]{1,0:T(8,128)(2,1)} %copy-done.28, bf16[768,512]{1,0:T(8,128)(2,1)} %copy-done.29, bf16[768,512]{1,0:T(8,128)(2,1)} %copy-done.29, bf16[768,512]{1,0:T(8,128)(2,1)} %copy-done.17, ...), custom_call_target="tpu_custom_call" | custom-call | flops 7247757312 | bytes 7077888 | tf_op jit(solution)/shard_map/combine/pallas_call | solution.py:424
  265.0 3.6 %collective-permute-done.23.refs_1_ = bf16[768,512]{1,0:T(8,128)(2,1)S(1)} collective-permute-done((bf16[768,512]{1,0:T(8,128)(2,1)S(1)}, bf16[768,512]{1,0:T(8,128)(2,1)S(1)}, u32[]{:S(2)}, u32[]{:S(2)}) %collective-permute-start.23) | collective-permute-done | bytes 786464 | tf_op jit(solution)/shard_map/ppermute | solution.py:158
  268.6 0.9 copy-done.18
  269.4 5.2 %combine.3 = bf16[512,1536]{1,0:T(8,128)(2,1)} custom-call(s32[54]{0:T(128)} %copy-done.12, bf16[768,512]{1,0:T(8,128)(2,1)} %copy-done.14, bf16[768,512]{1,0:T(8,128)(2,1)} %copy-done.18, bf16[8,3,96,1536]{3,2,1,0:T(8,128)(2,1)} %bitcast.61, bf16[512,1536]{1,0:T(8,128)(2,1)} %combine.2.refs_3_), custom_call_target="tpu_custom_call" | custom-call | flops 2415919104 | bytes 2359296 | tf_op jit(solution)/shard_map/combine/pallas_call | solution.py:424
  (120 shorter events, 8.1 us)
Async XLA Ops:
  7.2 10.0 %copy-start = (bf16[512,1536]{1,0:T(8,128)(2,1)S(1)}, bf16[512,1536]{1,0:T(8,128)(2,1)}, u32[]{:S(2)}) copy-start(bf16[512,1536]{1,0:T(8,128)(2,1)} %refs_0_.1) | copy-start | bytes 4718596
  7.2 16.5 %copy-start.27 = (s32[32]{0:T(128)S(1)}, s32[32]{0:T(128)}, u32[]{:S(2)}) copy-start(s32[32]{0:T(128)} %param.12) | copy-start | bytes 388
  7.2 16.8 %copy-start.26 = (s32[512]{0:T(512)S(1)}, s32[512]{0:T(512)}, u32[]{:S(2)}) copy-start(s32[512]{0:T(512)} %param.13) | copy-start | bytes 6148
  7.2 44.2 %copy-start.30 = (s32[32]{0:T(128)S(1)}, s32[32]{0:T(128)}, u32[]{:S(2)}) copy-start(s32[32]{0:T(128)} %param.15) | copy-start | bytes 388
  7.2 246.1 %all-gather.3.cloned.1.call-start = ((), (), s32[]{:S(2)}) async-start(), calls=%async_computation | async-start | bytes 7962624 | tf_op jit(solution)/shard_map/all_gather | solution.py:581
  7.2 39.8 %collective-permute-start.2 = (bf16[512,1536]{1,0:T(8,128)(2,1)}, bf16[512,1536]{1,0:T(8,128)(2,1)}, u32[]{:S(2)}, u32[]{:S(2)}) collective-permute-start(bf16[512,1536]{1,0:T(8,128)(2,1)} %refs_0_.1), channel_id=1, source_target_pairs={{3,2},{2,1},{1,0},{7,6},{6,5},{5,4},{11,10},{10,9},{9,8},{15,14},{... | collective-permute-start | bytes 4718600 | tf_op jit(solution)/shard_map/ppermute | solution.py:139
  8.7 39.7 %collective-permute-start = (bf16[512,1536]{1,0:T(8,128)(2,1)}, bf16[512,1536]{1,0:T(8,128)(2,1)}, u32[]{:S(2)}, u32[]{:S(2)}) collective-permute-start(bf16[512,1536]{1,0:T(8,128)(2,1)} %refs_0_.1), channel_id=1, source_target_pairs={{0,1},{1,2},{2,3},{4,5},{5,6},{6,7},{8,9},{9,10},{10,11},{12,13},{... | collective-permute-start | bytes 4718600 | tf_op jit(solution)/shard_map/ppermute | solution.py:139
  17.7 36.8 %collective-permute-start.5 = (f32[2,512]{1,0:T(2,128)S(1)}, f32[2,512]{1,0:T(2,128)S(1)}, u32[]{:S(2)}, u32[]{:S(2)}) collective-permute-start(f32[2,512]{1,0:T(2,128)S(1)} %get-tuple-element.31), channel_id=1, source_target_pairs={{0,1},{1,2},{2,3},{3,0},{4,5},{5,6},{6,7},{7,4},{8,9},{9,10},{10,1... | collective-permute-start | bytes 12296 | tf_op jit(solution)/shard_map/ppermute | solution.py:135
  18.6 35.9 %collective-permute-start.6 = (f32[2,512]{1,0:T(2,128)S(1)}, f32[2,512]{1,0:T(2,128)S(1)}, u32[]{:S(2)}, u32[]{:S(2)}) collective-permute-start(f32[2,512]{1,0:T(2,128)S(1)} %get-tuple-element.31), channel_id=1, source_target_pairs={{0,2},{1,3},{2,0},{3,1},{4,6},{5,7},{6,4},{7,5},{8,10},{9,11},{10,... | collective-permute-start | bytes 12296 | tf_op jit(solution)/shard_map/ppermute | solution.py:135
  20.8 33.8 %collective-permute-start.7 = (f32[2,512]{1,0:T(2,128)S(1)}, f32[2,512]{1,0:T(2,128)S(1)}, u32[]{:S(2)}, u32[]{:S(2)}) collective-permute-start(f32[2,512]{1,0:T(2,128)S(1)} %get-tuple-element.31), channel_id=1, source_target_pairs={{0,3},{1,0},{2,1},{3,2},{4,7},{5,4},{6,5},{7,6},{8,11},{9,8},{10,9... | collective-permute-start | bytes 12296 | tf_op jit(solution)/shard_map/ppermute | solution.py:135
  47.1 37.7 %collective-permute-start.3 = (bf16[512,1536]{1,0:T(8,128)(2,1)}, bf16[512,1536]{1,0:T(8,128)(2,1)}, u32[]{:S(2)}, u32[]{:S(2)}) collective-permute-start(bf16[512,1536]{1,0:T(8,128)(2,1)} %collective-permute-done.2.refs_1_.refs_0_), channel_id=1, source_target_pairs={{2,1},{1,0},{6,5},{5,4},{10,9},{9,8},{14,13},{13,12},{18,17},{17,1... | collective-permute-start | bytes 4718600 | tf_op jit(solution)/shard_map/ppermute | solution.py:139
  48.4 36.4 %collective-permute-start.1 = (bf16[512,1536]{1,0:T(8,128)(2,1)}, bf16[512,1536]{1,0:T(8,128)(2,1)}, u32[]{:S(2)}, u32[]{:S(2)}) collective-permute-start(bf16[512,1536]{1,0:T(8,128)(2,1)} %collective-permute-done.refs_0_), channel_id=1, source_target_pairs={{1,2},{2,3},{5,6},{6,7},{9,10},{10,11},{13,14},{14,15},{17,18},{18... | collective-permute-start | bytes 4718600 | tf_op jit(solution)/shard_map/ppermute | solution.py:139
  54.5 110.2 %copy-start.12 = (s32[54]{0:T(128)}, s32[54]{0:T(128)S(1)}, u32[]{:S(2)}) copy-start(s32[54]{0:T(128)S(1)} %concatenate.9.facts_ref) | copy-start | bytes 652
  86.4 37.2 %collective-permute-start.4 = (bf16[512,1536]{1,0:T(8,128)(2,1)S(1)}, bf16[512,1536]{1,0:T(8,128)(2,1)S(1)}, u32[]{:S(2)}, u32[]{:S(2)}) collective-permute-start(bf16[512,1536]{1,0:T(8,128)(2,1)S(1)} %broadcast_select_fusion.refs_0_), channel_id=1, source_target_pairs={{2,3},{1,0},{6,7},{5,4},{10,11},{9,8},{14,15},{13,12},{18,19},{17,... | collective-permute-start | bytes 4718600 | tf_op jit(solution)/shard_map/ppermute | solution.py:158
  99.3 25.4 %copy-start.8 = (bf16[96,1536]{1,0:T(8,128)(2,1)S(1)}, bf16[96,1536]{1,0:T(8,128)(2,1)}, u32[]{:S(2)}) copy-start(bf16[96,1536]{1,0:T(8,128)(2,1)} %get-tuple-element.16.refs_11_) | copy-start | bytes 884740
  99.3 25.4 %copy-start.9 = (bf16[96,1536]{1,0:T(8,128)(2,1)S(1)}, bf16[96,1536]{1,0:T(8,128)(2,1)}, u32[]{:S(2)}) copy-start(bf16[96,1536]{1,0:T(8,128)(2,1)} %get-tuple-element.15.refs_10_) | copy-start | bytes 884740
  99.3 25.4 %copy-start.10 = (bf16[96,1536]{1,0:T(8,128)(2,1)S(1)}, bf16[96,1536]{1,0:T(8,128)(2,1)}, u32[]{:S(2)}) copy-start(bf16[96,1536]{1,0:T(8,128)(2,1)} %get-tuple-element.14.refs_9_) | copy-start | bytes 884740
  134.0 46.6 %copy-start.3 = (bf16[288,512]{1,0:T(8,128)(2,1)}, bf16[288,512]{1,0:T(8,128)(2,1)S(1)}, u32[]{:S(2)}) copy-start(bf16[288,512]{1,0:T(8,128)(2,1)S(1)} %get-tuple-element.17.refs_0_) | copy-start | bytes 884740
  134.0 46.6 %copy-start.4 = (bf16[4,288,512]{2,1,0:T(8,128)(2,1)}, bf16[4,288,512]{2,1,0:T(8,128)(2,1)S(1)}, u32[]{:S(2)}) copy-start(bf16[4,288,512]{2,1,0:T(8,128)(2,1)S(1)} %get-tuple-element.18.refs_4_) | copy-start | bytes 3538948
  134.1 46.5 %copy-start.5 = (bf16[288,512]{1,0:T(8,128)(2,1)}, bf16[288,512]{1,0:T(8,128)(2,1)S(1)}, u32[]{:S(2)}) copy-start(bf16[288,512]{1,0:T(8,128)(2,1)S(1)} %get-tuple-element.19.refs_1_) | copy-start | bytes 884740
  134.1 46.5 %copy-start.6 = (bf16[288,512]{1,0:T(8,128)(2,1)}, bf16[288,512]{1,0:T(8,128)(2,1)S(1)}, u32[]{:S(2)}) copy-start(bf16[288,512]{1,0:T(8,128)(2,1)S(1)} %get-tuple-element.20.refs_2_) | copy-start | bytes 884740
  134.1 46.5 %copy-start.7 = (bf16[288,512]{1,0:T(8,128)(2,1)}, bf16[288,512]{1,0:T(8,128)(2,1)S(1)}, u32[]{:S(2)}) copy-start(bf16[288,512]{1,0:T(8,128)(2,1)S(1)} %get-tuple-element.21.refs_3_) | copy-start | bytes 884740
  134.1 30.7 %copy-start.13 = (s32[8,8]{1,0:T(8,128)S(1)}, s32[8,8]{1,0:T(8,128)}, u32[]{:S(2)}) copy-start(s32[8,8]{1,0:T(8,128)} %pair_ref.1) | copy-start | bytes 772
  134.1 3.6 %collective-permute-start.8 = (bf16[4,288,512]{2,1,0:T(8,128)(2,1)S(1)}, bf16[4,288,512]{2,1,0:T(8,128)(2,1)S(1)}, u32[]{:S(2)}, u32[]{:S(2)}) collective-permute-start(bf16[4,288,512]{2,1,0:T(8,128)(2,1)S(1)} %get-tuple-element.18.refs_4_), channel_id=1, source_target_pairs={{0,4},{4,0},{8,12},{12,8},{16,20},{20,16},{24,28},{28,24},{1,5},{5... | collective-permute-start | bytes 3538952 | tf_op jit(solution)/shard_map/ppermute | solution.py:336
  134.2 16.2 %collective-permute-start.11 = (bf16[288,512]{1,0:T(8,128)(2,1)S(1)}, bf16[288,512]{1,0:T(8,128)(2,1)S(1)}, u32[]{:S(2)}, u32[]{:S(2)}) collective-permute-start(bf16[288,512]{1,0:T(8,128)(2,1)S(1)} %get-tuple-element.20.refs_2_), channel_id=1, source_target_pairs={{0,16},{4,20},{8,24},{12,28},{16,0},{20,4},{24,8},{28,12},{1,17},{... | collective-permute-start | bytes 884744 | tf_op jit(solution)/shard_map/ppermute | solution.py:336
  135.8 17.1 %collective-permute-start.13 = (bf16[288,512]{1,0:T(8,128)(2,1)S(1)}, bf16[288,512]{1,0:T(8,128)(2,1)S(1)}, u32[]{:S(2)}, u32[]{:S(2)}) collective-permute-start(bf16[288,512]{1,0:T(8,128)(2,1)S(1)} %get-tuple-element.21.refs_3_), channel_id=1, source_target_pairs={{0,24},{4,28},{8,16},{12,20},{16,8},{20,12},{24,0},{28,4},{1,25},{... | collective-permute-start | bytes 884744 | tf_op jit(solution)/shard_map/ppermute | solution.py:336
  137.2 15.6 %collective-permute-start.9 = (bf16[288,512]{1,0:T(8,128)(2,1)S(1)}, bf16[288,512]{1,0:T(8,128)(2,1)S(1)}, u32[]{:S(2)}, u32[]{:S(2)}) collective-permute-start(bf16[288,512]{1,0:T(8,128)(2,1)S(1)} %get-tuple-element.19.refs_1_), channel_id=1, source_target_pairs={{0,8},{4,12},{8,0},{12,4},{16,24},{20,28},{24,16},{28,20},{1,9},{5... | collective-permute-start | bytes 884744 | tf_op jit(solution)/shard_map/ppermute | solution.py:336
  137.8 20.6 %collective-permute-start.10 = (bf16[288,512]{1,0:T(8,128)(2,1)S(1)}, bf16[288,512]{1,0:T(8,128)(2,1)S(1)}, u32[]{:S(2)}, u32[]{:S(2)}) collective-permute-start(bf16[288,512]{1,0:T(8,128)(2,1)S(1)} %get-tuple-element.28), channel_id=1, source_target_pairs={{0,8},{4,12},{8,0},{12,4},{16,24},{20,28},{24,16},{28,20},{1,9},{5... | collective-permute-start | bytes 884744 | tf_op jit(solution)/shard_map/ppermute | solution.py:336
  139.4 23.9 %collective-permute-start.12 = (bf16[288,512]{1,0:T(8,128)(2,1)S(1)}, bf16[288,512]{1,0:T(8,128)(2,1)S(1)}, u32[]{:S(2)}, u32[]{:S(2)}) collective-permute-start(bf16[288,512]{1,0:T(8,128)(2,1)S(1)} %get-tuple-element.27), channel_id=1, source_target_pairs={{0,16},{4,20},{8,24},{12,28},{16,0},{20,4},{24,8},{28,12},{1,17},{... | collective-permute-start | bytes 884744 | tf_op jit(solution)/shard_map/ppermute | solution.py:336
  150.4 14.4 %collective-permute-start.14 = (bf16[288,512]{1,0:T(8,128)(2,1)S(1)}, bf16[288,512]{1,0:T(8,128)(2,1)S(1)}, u32[]{:S(2)}, u32[]{:S(2)}) collective-permute-start(bf16[288,512]{1,0:T(8,128)(2,1)S(1)} %get-tuple-element.26), channel_id=1, source_target_pairs={{0,24},{4,28},{8,16},{12,20},{16,8},{20,12},{24,0},{28,4},{1,25},{... | collective-permute-start | bytes 884744 | tf_op jit(solution)/shard_map/ppermute | solution.py:336
  152.8 28.5 %collective-permute-start.24 = (bf16[96,1536]{1,0:T(8,128)(2,1)S(1)}, bf16[96,1536]{1,0:T(8,128)(2,1)S(1)}, u32[]{:S(2)}, u32[]{:S(2)}) collective-permute-start(bf16[96,1536]{1,0:T(8,128)(2,1)S(1)} %copy-done.10), channel_id=1, source_target_pairs={{0,1},{1,2},{2,3},{3,0},{4,5},{5,6},{6,7},{7,4},{8,9},{9,10},{10,1... | collective-permute-start | bytes 884744 | tf_op jit(solution)/shard_map/ppermute | solution.py:135
  152.8 28.5 %collective-permute-start.25 = (bf16[96,1536]{1,0:T(8,128)(2,1)S(1)}, bf16[96,1536]{1,0:T(8,128)(2,1)S(1)}, u32[]{:S(2)}, u32[]{:S(2)}) collective-permute-start(bf16[96,1536]{1,0:T(8,128)(2,1)S(1)} %copy-done.9), channel_id=1, source_target_pairs={{0,2},{1,3},{2,0},{3,1},{4,6},{5,7},{6,4},{7,5},{8,10},{9,11},{10,... | collective-permute-start | bytes 884744 | tf_op jit(solution)/shard_map/ppermute | solution.py:135
  158.4 22.9 %collective-permute-start.26 = (bf16[96,1536]{1,0:T(8,128)(2,1)S(1)}, bf16[96,1536]{1,0:T(8,128)(2,1)S(1)}, u32[]{:S(2)}, u32[]{:S(2)}) collective-permute-start(bf16[96,1536]{1,0:T(8,128)(2,1)S(1)} %copy-done.8), channel_id=1, source_target_pairs={{0,3},{1,0},{2,1},{3,2},{4,7},{5,4},{6,5},{7,6},{8,11},{9,8},{10,9... | collective-permute-start | bytes 884744 | tf_op jit(solution)/shard_map/ppermute | solution.py:135
  181.3 7.3 %copy-start.2 = (bf16[2,96,512]{2,1,0:T(8,128)(2,1)S(1)}, bf16[2,96,512]{2,1,0:T(8,128)(2,1)}, u32[]{:S(2)}) copy-start(bf16[2,96,512]{2,1,0:T(8,128)(2,1)} %copy-done.1) | copy-start | bytes 589828
  185.0 8.8 %collective-permute-start.17 = (bf16[2,96,512]{2,1,0:T(8,128)(2,1)S(1)}, bf16[2,96,512]{2,1,0:T(8,128)(2,1)S(1)}, u32[]{:S(2)}, u32[]{:S(2)}) collective-permute-start(bf16[2,96,512]{2,1,0:T(8,128)(2,1)S(1)} %get-tuple-element.25), channel_id=1, source_target_pairs={{0,24},{4,28},{8,16},{12,20},{16,8},{20,12},{24,0},{28,4},{1,25},{... | collective-permute-start | bytes 589832 | tf_op jit(solution)/shard_map/ppermute | solution.py:336
  186.6 9.8 %collective-permute-start.16 = (bf16[2,96,512]{2,1,0:T(8,128)(2,1)S(1)}, bf16[2,96,512]{2,1,0:T(8,128)(2,1)S(1)}, u32[]{:S(2)}, u32[]{:S(2)}) collective-permute-start(bf16[2,96,512]{2,1,0:T(8,128)(2,1)S(1)} %get-tuple-element.24), channel_id=1, source_target_pairs={{0,16},{4,20},{8,24},{12,28},{16,0},{20,4},{24,8},{28,12},{1,17},{... | collective-permute-start | bytes 589832 | tf_op jit(solution)/shard_map/ppermute | solution.py:336
  188.0 8.3 %collective-permute-start.15 = (bf16[2,96,512]{2,1,0:T(8,128)(2,1)S(1)}, bf16[2,96,512]{2,1,0:T(8,128)(2,1)S(1)}, u32[]{:S(2)}, u32[]{:S(2)}) collective-permute-start(bf16[2,96,512]{2,1,0:T(8,128)(2,1)S(1)} %get-tuple-element.23), channel_id=1, source_target_pairs={{0,8},{4,12},{8,0},{12,4},{16,24},{20,28},{24,16},{28,20},{1,9},{5... | collective-permute-start | bytes 589832 | tf_op jit(solution)/shard_map/ppermute | solution.py:336
  193.9 4.4 %copy-start.19 = (bf16[2,96,512]{2,1,0:T(8,128)(2,1)}, bf16[2,96,512]{2,1,0:T(8,128)(2,1)S(1)}, u32[]{:S(2)}) copy-start(bf16[2,96,512]{2,1,0:T(8,128)(2,1)S(1)} %collective-permute-done.17.refs_3_) | copy-start | bytes 589828
  196.5 1.8 collective-permute-start.18
  201.3 20.6 %collective-permute-start.19 = (bf16[768,512]{1,0:T(8,128)(2,1)}, bf16[768,512]{1,0:T(8,128)(2,1)S(1)}, u32[]{:S(2)}, u32[]{:S(2)}) collective-permute-start(bf16[768,512]{1,0:T(8,128)(2,1)} %bitcast.62), channel_id=1, source_target_pairs={{0,1},{1,2},{2,3},{4,5},{5,6},{6,7},{8,9},{9,10},{10,11},{12,13},{... | collective-permute-start | bytes 2359304 | tf_op jit(solution)/shard_map/ppermute | solution.py:139
  204.6 22.0 %collective-permute-start.21 = (bf16[768,512]{1,0:T(8,128)(2,1)}, bf16[768,512]{1,0:T(8,128)(2,1)S(1)}, u32[]{:S(2)}, u32[]{:S(2)}) collective-permute-start(bf16[768,512]{1,0:T(8,128)(2,1)} %bitcast.63), channel_id=1, source_target_pairs={{3,2},{2,1},{1,0},{7,6},{6,5},{5,4},{11,10},{10,9},{9,8},{15,14},{... | collective-permute-start | bytes 2359304 | tf_op jit(solution)/shard_map/ppermute | solution.py:139
  221.9 6.0 %copy-start.28 = (bf16[768,512]{1,0:T(8,128)(2,1)}, bf16[768,512]{1,0:T(8,128)(2,1)S(1)}, u32[]{:S(2)}) copy-start(bf16[768,512]{1,0:T(8,128)(2,1)S(1)} %collective-permute-done.19.refs_1_) | copy-start | bytes 2359300
  221.9 5.9 %collective-permute-start.20 = (bf16[768,512]{1,0:T(8,128)(2,1)S(1)}, bf16[768,512]{1,0:T(8,128)(2,1)S(1)}, u32[]{:S(2)}, u32[]{:S(2)}) collective-permute-start(bf16[768,512]{1,0:T(8,128)(2,1)S(1)} %collective-permute-done.19.refs_1_), channel_id=1, source_target_pairs={{1,2},{2,3},{5,6},{6,7},{9,10},{10,11},{13,14},{14,15},{17,18},{18... | collective-permute-start | bytes 2359304 | tf_op jit(solution)/shard_map/ppermute | solution.py:139
  226.6 21.7 %collective-permute-start.22 = (bf16[768,512]{1,0:T(8,128)(2,1)S(1)}, bf16[768,512]{1,0:T(8,128)(2,1)S(1)}, u32[]{:S(2)}, u32[]{:S(2)}) collective-permute-start(bf16[768,512]{1,0:T(8,128)(2,1)S(1)} %collective-permute-done.21.refs_2_.refs_3_), channel_id=1, source_target_pairs={{2,1},{1,0},{6,5},{5,4},{10,9},{9,8},{14,13},{13,12},{18,17},{17,1... | collective-permute-start | bytes 2359304 | tf_op jit(solution)/shard_map/ppermute | solution.py:139
  227.9 25.4 %copy-start.16 = (bf16[768,512]{1,0:T(8,128)(2,1)}, bf16[768,512]{1,0:T(8,128)(2,1)S(1)}, u32[]{:S(2)}) copy-start(bf16[768,512]{1,0:T(8,128)(2,1)S(1)} %collective-permute-done.20.refs_5_) | copy-start | bytes 2359300
  248.3 5.0 %copy-start.17 = (bf16[768,512]{1,0:T(8,128)(2,1)}, bf16[768,512]{1,0:T(8,128)(2,1)S(1)}, u32[]{:S(2)}) copy-start(bf16[768,512]{1,0:T(8,128)(2,1)S(1)} %collective-permute-done.22.refs_4_) | copy-start | bytes 2359300
  248.4 4.9 %copy-start.14 = (bf16[768,512]{1,0:T(8,128)(2,1)}, bf16[768,512]{1,0:T(8,128)(2,1)S(1)}, u32[]{:S(2)}) copy-start(bf16[768,512]{1,0:T(8,128)(2,1)S(1)} %broadcast_select_fusion.1.refs_0_) | copy-start | bytes 2359300
  248.4 20.1 %collective-permute-start.23 = (bf16[768,512]{1,0:T(8,128)(2,1)S(1)}, bf16[768,512]{1,0:T(8,128)(2,1)S(1)}, u32[]{:S(2)}, u32[]{:S(2)}) collective-permute-start(bf16[768,512]{1,0:T(8,128)(2,1)S(1)} %broadcast_select_fusion.1.refs_0_), channel_id=1, source_target_pairs={{2,3},{1,0},{6,7},{5,4},{10,11},{9,8},{14,15},{13,12},{18,19},{17,... | collective-permute-start | bytes 2359304 | tf_op jit(solution)/shard_map/ppermute | solution.py:158
  (11 other events, 14.3 us)
Sparse Core Ops, SparseCore 0:
  185.2 50.9 all-gather.2

commit v2 on v1

--- a/solution.py
+++ b/solution.py
@@ -578,8 +578,8 @@
 
     columns = [turn(window, distance) for distance, window in zip((1, 2, 3), windows)]
     mixed = list(attend(facts, pair_table, start, arrived))
-    others = lax.all_gather(stack(columns, mixed[:1]), "blk", axis=0)
     heads = to_blocks(facts, mixed)
+    others = lax.all_gather(stack(columns, [heads]), "blk", axis=0)
 
     came, result = [], [None]
 

time: 283 us -> 305 us (1.078)
  waiting for transfers between devices: 120 us -> 142 us
    ppermute x6, waiting for transfers between devices: 0.02 us -> 16.3 us  [turn(): lax.ppermute(value, 'tp', [(source, (source + distance) % 4) for source i...]
    ppermute x11, waiting for transfers between devices: 20.4 us -> 29.1 us  [swap(): lax.ppermute(value, 'blk', [(place, place ^ distance) for place in range(...]
    ppermute x8, starting transfers between devices: 17.8 us -> 23.3 us  [line_hop(): return (lax.ppermute(up, 'tp', ups), lax.ppermute(down, 'tp', downs))]
    ppermute x6, starting transfers between devices: 16.4 us -> 12 us  [turn(): lax.ppermute(value, 'tp', [(source, (source + distance) % 4) for source i...]
  transfers between devices with their start and end apart: 28 -> 28, of which waited for: 12 -> 14; matrix products, arithmetic and copies ran while one was open for 2% -> 2% of each run, Pallas kernels for 24% -> 17%
where the time goes in v2:
time: 305 us; the launch traced here: 304 us
  waiting for transfers between devices  142 us (47%)
  Pallas kernels  85.8 us (28%)
  starting transfers between devices  51.1 us (17%)
  between operations  14.8 us (5%)
  other arithmetic  5.32 us (2%)
  local copies, waits for them, and re-layouts  4.61 us (2%)
    ppermute x8, waiting for transfers between devices, line_hop(): return (lax.ppermute(up, 'tp', ups), lax.ppermute(down, 'tp', downs))  81.6 us
    pallas_call x4, Pallas kernels, project(): pl.pallas_call(functools.partial(project_kernel, step, len(shards)), grid...  41.7 us
    ppermute x11, waiting for transfers between devices, swap(): lax.ppermute(value, 'blk', [(place, place ^ distance) for place in range(...  29.1 us
    ppermute x8, starting transfers between devices, line_hop(): return (lax.ppermute(up, 'tp', ups), lax.ppermute(down, 'tp', downs))  23.3 us
    pallas_call x2, Pallas kernels, combine(): pl.pallas_call(functools.partial(combine_kernel, steps, tuple((len(step)...  16.9 us
    pallas_call x1, Pallas kernels, attend(): pl.pallas_call(attend_kernel, in_specs=[smem, smem, vmem] + [vmem] * len(...  16.4 us
    ppermute x6, waiting for transfers between devices, turn(): lax.ppermute(value, 'tp', [(source, (source + distance) % 4) for source i...  16.3 us
    ppermute x2, waiting for transfers between devices, gather_line(): outer = lax.ppermute(inner, 'tp', [(2, 3), (1, 0)])  15.2 us
  transfers between devices with their start and end apart: 28, of which 14 were waited for; matrix products, arithmetic and copies ran while one was open for 2% of the time, Pallas kernels for 17%

profile of v2, /device:TPU:0, one launch (start us, length us, event | category | flops | bytes accessed | tf_op | source)
XLA Modules:
  0.0 303.8 jit_solution(13952970464647136346)
XLA Ops:
  7.2 1.4 collective-permute-start.2
  8.7 6.8 %collective-permute-start = (bf16[512,1536]{1,0:T(8,128)(2,1)}, bf16[512,1536]{1,0:T(8,128)(2,1)}, u32[]{:S(2)}, u32[]{:S(2)}) collective-permute-start(bf16[512,1536]{1,0:T(8,128)(2,1)} %refs_0_.1), channel_id=1, source_target_pairs={{0,1},{1,2},{2,3},{4,5},{5,6},{6,7},{8,9},{9,10},{10,11},{12,13},{... | collective-permute-start | bytes 4718600 | tf_op jit(solution)/shard_map/ppermute | solution.py:139
  15.5 1.7 convert_reduce_fusion
  18.6 2.2 collective-permute-start.6
  20.8 2.8 collective-permute-start.7
  24.3 22.8 %collective-permute-done.2.refs_1_.refs_0_ = bf16[512,1536]{1,0:T(8,128)(2,1)} collective-permute-done((bf16[512,1536]{1,0:T(8,128)(2,1)}, bf16[512,1536]{1,0:T(8,128)(2,1)}, u32[]{:S(2)}, u32[]{:S(2)}) %collective-permute-start.2) | collective-permute-done | bytes 1572896 | tf_op jit(solution)/shard_map/ppermute | solution.py:139
  47.1 1.3 collective-permute-start.3
  48.4 1.8 collective-permute-start.1
  51.5 2.9 shares.1
  55.0 9.0 %project.4.refs_6_ = f32[3,512,768]{2,1,0:T(8,128)} custom-call(s32[54]{0:T(128)S(1)} %concatenate.9.facts_ref, bf16[512,1536]{1,0:T(8,128)(2,1)S(1)} %copy-done, f32[512,1]{1,0:T(8,128)S(1)} %copy.42.refs_1_.refs_2_.refs_3_, f32[512,1]{1,0:T(8,128)S(1)} %copy.43.refs_2_.refs_3_.refs_4_, f32[4,1,1536]{2,1,0:T(1,128)S(1)} %bitcast.50, ...), custom_call_target="tpu_custom_call" | custom-call | flops 603979776 | tf_op jit(solution)/shard_map/project/pallas_call | solution.py:232
  64.0 20.8 %collective-permute-done.3.refs_1_ = bf16[512,1536]{1,0:T(8,128)(2,1)} collective-permute-done((bf16[512,1536]{1,0:T(8,128)(2,1)}, bf16[512,1536]{1,0:T(8,128)(2,1)}, u32[]{:S(2)}, u32[]{:S(2)}) %collective-permute-start.3) | collective-permute-done | bytes 1572896 | tf_op jit(solution)/shard_map/ppermute | solution.py:139
  84.8 1.6 broadcast_select_fusion.refs_0_
  86.4 1.5 collective-permute-start.4
  87.9 11.4 %project.5.refs_7_ = f32[3,512,768]{2,1,0:T(8,128)} custom-call(s32[54]{0:T(128)S(1)} %concatenate.9.facts_ref, bf16[512,1536]{1,0:T(8,128)(2,1)} %collective-permute-done.refs_0_, bf16[512,1536]{1,0:T(8,128)(2,1)} %collective-permute-done.2.refs_1_.refs_0_, f32[512,1]{1,0:T(8,128)S(1)} %copy.42.refs_1_.refs_2_.refs_3_, ...), custom_call_target="tpu_custom_call" | custom-call | flops 12079595520 | tf_op jit(solution)/shard_map/project/pallas_call | solution.py:232
  99.3 11.9 %project.6.refs_6_ = f32[3,512,768]{2,1,0:T(8,128)} custom-call(s32[54]{0:T(128)S(1)} %concatenate.9.facts_ref, bf16[512,1536]{1,0:T(8,128)(2,1)} %collective-permute-done.2.refs_1_.refs_0_, bf16[512,1536]{1,0:T(8,128)(2,1)} %collective-permute-done.3.refs_1_, bf16[512,1536]{1,0:T(8,128)(2,1)} %collective-permute-done.1.refs_2_, ...), custom_call_target="tpu_custom_call" | custom-call | flops 12079595520 | tf_op jit(solution)/shard_map/project/pallas_call | solution.py:232
  111.2 12.3 %collective-permute-done.4.refs_1_ = bf16[512,1536]{1,0:T(8,128)(2,1)S(1)} collective-permute-done((bf16[512,1536]{1,0:T(8,128)(2,1)S(1)}, bf16[512,1536]{1,0:T(8,128)(2,1)S(1)}, u32[]{:S(2)}, u32[]{:S(2)}) %collective-permute-start.4) | collective-permute-done | bytes 1572896 | tf_op jit(solution)/shard_map/ppermute | solution.py:158
  123.5 1.1 copy-done.16
  124.7 9.3 %project.7 = (bf16[288,512]{1,0:T(8,128)(2,1)S(1)}, bf16[288,512]{1,0:T(8,128)(2,1)S(1)}, bf16[288,512]{1,0:T(8,128)(2,1)S(1)}, bf16[288,512]{1,0:T(8,128)(2,1)S(1)}, bf16[4,288,512]{2,1,0:T(8,128)(2,1)S(1)}) custom-call(s32[54]{0:T(128)S(1)} %concatenate.9.facts_ref, bf16[512,1536]{1,0:T(8,128)(2,1)S(1)} %broadcast_select_fusion.refs_0_, ...), custom_call_target="tpu_custom_call" | custom-call | flops 3623878656 | tf_op jit(solution)/shard_map/project/pallas_call | solution.py:232
  134.2 1.6 collective-permute-start.11
  135.8 1.4 collective-permute-start.13
  137.8 1.6 collective-permute-start.10
  139.4 1.5 collective-permute-start.12
  140.9 9.5 %collective-permute-done.11.refs_4_ = bf16[288,512]{1,0:T(8,128)(2,1)S(1)} collective-permute-done((bf16[288,512]{1,0:T(8,128)(2,1)S(1)}, bf16[288,512]{1,0:T(8,128)(2,1)S(1)}, u32[]{:S(2)}, u32[]{:S(2)}) %collective-permute-start.11) | collective-permute-done | bytes 294944 | tf_op jit(solution)/shard_map/ppermute | solution.py:336
  150.4 2.4 collective-permute-start.14
  152.8 5.4 %collective-permute-done.10.refs_3_ = bf16[288,512]{1,0:T(8,128)(2,1)S(1)} collective-permute-done((bf16[288,512]{1,0:T(8,128)(2,1)S(1)}, bf16[288,512]{1,0:T(8,128)(2,1)S(1)}, u32[]{:S(2)}, u32[]{:S(2)}) %collective-permute-start.10) | collective-permute-done | bytes 294944 | tf_op jit(solution)/shard_map/ppermute | solution.py:336
  158.2 6.5 %collective-permute-done.14.refs_7_ = bf16[288,512]{1,0:T(8,128)(2,1)S(1)} collective-permute-done((bf16[288,512]{1,0:T(8,128)(2,1)S(1)}, bf16[288,512]{1,0:T(8,128)(2,1)S(1)}, u32[]{:S(2)}, u32[]{:S(2)}) %collective-permute-start.14) | collective-permute-done | bytes 294944 | tf_op jit(solution)/shard_map/ppermute | solution.py:336
  164.8 16.4 %attend.1 = (bf16[2,96,512]{2,1,0:T(8,128)(2,1)S(1)}, bf16[2,96,512]{2,1,0:T(8,128)(2,1)S(1)}, bf16[2,96,512]{2,1,0:T(8,128)(2,1)S(1)}, bf16[2,96,512]{2,1,0:T(8,128)(2,1)S(1)}) custom-call(s32[54]{0:T(128)S(1)} %concatenate.9.facts_ref, s32[8,8]{1,0:T(8,128)S(1)} %copy-done.13, s32[8,1,512]{2,1,0:T(1,128)S(1)} %bitcast.55, ...), custom_call_target="tpu_custom_call" | custom-call | flops 1000 | bytes 1000 | tf_op jit(solution)/shard_map/attend/pallas_call | solution.py:315
  181.2 1.5 collective-permute-start.17
  182.7 1.5 collective-permute-start.16
  184.8 5.3 %collective-permute-done.17.refs_3_ = bf16[2,96,512]{2,1,0:T(8,128)(2,1)S(1)} collective-permute-done((bf16[2,96,512]{2,1,0:T(8,128)(2,1)S(1)}, bf16[2,96,512]{2,1,0:T(8,128)(2,1)S(1)}, u32[]{:S(2)}, u32[]{:S(2)}) %collective-permute-start.17) | collective-permute-done | bytes 196640 | tf_op jit(solution)/shard_map/ppermute | solution.py:336
  190.1 2.5 collective-permute-done.16.refs_2_
  192.8 5.6 %collective-permute-start.25 = (bf16[96,1536]{1,0:T(8,128)(2,1)S(1)}, bf16[96,1536]{1,0:T(8,128)(2,1)S(1)}, u32[]{:S(2)}, u32[]{:S(2)}) collective-permute-start(bf16[96,1536]{1,0:T(8,128)(2,1)S(1)} %copy-done.9), channel_id=1, source_target_pairs={{0,2},{1,3},{2,0},{3,1},{4,6},{5,7},{6,4},{7,5},{8,10},{9,11},{10,... | collective-permute-start | bytes 884744 | tf_op jit(solution)/shard_map/ppermute | solution.py:135
  199.6 2.3 order.1
  201.9 3.9 %collective-permute-done.24.refs_0_ = bf16[96,1536]{1,0:T(8,128)(2,1)S(1)} collective-permute-done((bf16[96,1536]{1,0:T(8,128)(2,1)S(1)}, bf16[96,1536]{1,0:T(8,128)(2,1)S(1)}, u32[]{:S(2)}, u32[]{:S(2)}) %collective-permute-start.24) | collective-permute-done | bytes 294944 | tf_op jit(solution)/shard_map/ppermute | solution.py:135
  205.9 12.3 %collective-permute-done.25.refs_1_ = bf16[96,1536]{1,0:T(8,128)(2,1)S(1)} collective-permute-done((bf16[96,1536]{1,0:T(8,128)(2,1)S(1)}, bf16[96,1536]{1,0:T(8,128)(2,1)S(1)}, u32[]{:S(2)}, u32[]{:S(2)}) %collective-permute-start.25) | collective-permute-done | bytes 294944 | tf_op jit(solution)/shard_map/ppermute | solution.py:135
  219.0 2.3 stack.114
  221.3 8.7 %collective-permute-start.19 = (bf16[768,512]{1,0:T(8,128)(2,1)S(1)}, bf16[768,512]{1,0:T(8,128)(2,1)S(1)}, u32[]{:S(2)}, u32[]{:S(2)}) collective-permute-start(bf16[768,512]{1,0:T(8,128)(2,1)S(1)} %bitcast.64), channel_id=1, source_target_pairs={{0,1},{1,2},{2,3},{4,5},{5,6},{6,7},{8,9},{9,10},{10,11},{12,13},{... | collective-permute-start | bytes 2359304 | tf_op jit(solution)/shard_map/ppermute | solution.py:139
  230.0 1.3 collective-permute-start.21
  231.3 15.6 %collective-permute-done.19.refs_1_ = bf16[768,512]{1,0:T(8,128)(2,1)S(1)} collective-permute-done((bf16[768,512]{1,0:T(8,128)(2,1)S(1)}, bf16[768,512]{1,0:T(8,128)(2,1)S(1)}, u32[]{:S(2)}, u32[]{:S(2)}) %collective-permute-start.19) | collective-permute-done | bytes 786464 | tf_op jit(solution)/shard_map/ppermute | solution.py:139
  247.7 3.5 %collective-permute-done.21.refs_2_.refs_3_ = bf16[768,512]{1,0:T(8,128)(2,1)S(1)} collective-permute-done((bf16[768,512]{1,0:T(8,128)(2,1)S(1)}, bf16[768,512]{1,0:T(8,128)(2,1)S(1)}, u32[]{:S(2)}, u32[]{:S(2)}) %collective-permute-start.21) | collective-permute-done | bytes 786464 | tf_op jit(solution)/shard_map/ppermute | solution.py:139
  251.1 1.3 collective-permute-start.22
  252.5 18.9 %collective-permute-done.22.refs_4_ = bf16[768,512]{1,0:T(8,128)(2,1)S(1)} collective-permute-done((bf16[768,512]{1,0:T(8,128)(2,1)S(1)}, bf16[768,512]{1,0:T(8,128)(2,1)S(1)}, u32[]{:S(2)}, u32[]{:S(2)}) %collective-permute-start.22) | collective-permute-done | bytes 786464 | tf_op jit(solution)/shard_map/ppermute | solution.py:139
  271.4 1.5 collective-permute-start.23
  273.0 3.3 %pages.1 = bf16[2,32,16,768]{3,2,1,0:T(8,128)(2,1)} custom-call(s32[54]{0:T(128)} %copy-done.12, bf16[288,512]{1,0:T(8,128)(2,1)} %copy-done.1, bf16[288,512]{1,0:T(8,128)(2,1)} %copy-done.4, bf16[288,512]{1,0:T(8,128)(2,1)} %copy-done.5, bf16[288,512]{1,0:T(8,128)(2,1)} %copy-done.6, bf16[4,288,512]{2,1,0:T(8,128)(2,1)} %copy-done.2), custom_call_target="tpu_custom_call" | custom-call | bytes 10485760 | tf_op jit(solution)/shard_map/pages/pallas_call | solution.py:510
  276.3 11.6 %combine.2.refs_3_ = bf16[512,1536]{1,0:T(8,128)(2,1)} custom-call(s32[54]{0:T(128)} %copy-done.12, bf16[768,512]{1,0:T(8,128)(2,1)} %bitcast.63, bf16[768,512]{1,0:T(8,128)(2,1)} %copy-done.29, bf16[768,512]{1,0:T(8,128)(2,1)} %copy-done.30, bf16[768,512]{1,0:T(8,128)(2,1)} %copy-done.30, bf16[768,512]{1,0:T(8,128)(2,1)} %copy-done.18, ...), custom_call_target="tpu_custom_call" | custom-call | flops 7247757312 | bytes 7077888 | tf_op jit(solution)/shard_map/combine/pallas_call | solution.py:424
  288.0 2.9 collective-permute-done.23.refs_1_
  290.8 0.9 copy-done.19
  291.7 5.2 %combine.3 = bf16[512,1536]{1,0:T(8,128)(2,1)} custom-call(s32[54]{0:T(128)} %copy-done.12, bf16[768,512]{1,0:T(8,128)(2,1)} %copy-done.14, bf16[768,512]{1,0:T(8,128)(2,1)} %copy-done.19, bf16[8,3,96,1536]{3,2,1,0:T(8,128)(2,1)} %bitcast.61, bf16[512,1536]{1,0:T(8,128)(2,1)} %combine.2.refs_3_), custom_call_target="tpu_custom_call" | custom-call | flops 2415919104 | bytes 2359296 | tf_op jit(solution)/shard_map/combine/pallas_call | solution.py:424
  (122 shorter events, 8.0 us)
Async XLA Ops:
  7.2 10.0 %copy-start = (bf16[512,1536]{1,0:T(8,128)(2,1)S(1)}, bf16[512,1536]{1,0:T(8,128)(2,1)}, u32[]{:S(2)}) copy-start(bf16[512,1536]{1,0:T(8,128)(2,1)} %refs_0_.1) | copy-start | bytes 4718596
  7.2 16.5 %copy-start.28 = (s32[32]{0:T(128)S(1)}, s32[32]{0:T(128)}, u32[]{:S(2)}) copy-start(s32[32]{0:T(128)} %param.12) | copy-start | bytes 388
  7.2 16.8 %copy-start.27 = (s32[512]{0:T(512)S(1)}, s32[512]{0:T(512)}, u32[]{:S(2)}) copy-start(s32[512]{0:T(512)} %param.13) | copy-start | bytes 6148
  7.2 44.1 %copy-start.31 = (s32[32]{0:T(128)S(1)}, s32[32]{0:T(128)}, u32[]{:S(2)}) copy-start(s32[32]{0:T(128)} %param.15) | copy-start | bytes 388
  7.2 269.1 %all-gather.3.cloned.1.call-start = ((), (), s32[]{:S(2)}) async-start(), calls=%async_computation | async-start | bytes 7962624 | tf_op jit(solution)/shard_map/all_gather | solution.py:582
  7.2 39.8 %collective-permute-start.2 = (bf16[512,1536]{1,0:T(8,128)(2,1)}, bf16[512,1536]{1,0:T(8,128)(2,1)}, u32[]{:S(2)}, u32[]{:S(2)}) collective-permute-start(bf16[512,1536]{1,0:T(8,128)(2,1)} %refs_0_.1), channel_id=1, source_target_pairs={{3,2},{2,1},{1,0},{7,6},{6,5},{5,4},{11,10},{10,9},{9,8},{15,14},{... | collective-permute-start | bytes 4718600 | tf_op jit(solution)/shard_map/ppermute | solution.py:139
  8.7 39.7 %collective-permute-start = (bf16[512,1536]{1,0:T(8,128)(2,1)}, bf16[512,1536]{1,0:T(8,128)(2,1)}, u32[]{:S(2)}, u32[]{:S(2)}) collective-permute-start(bf16[512,1536]{1,0:T(8,128)(2,1)} %refs_0_.1), channel_id=1, source_target_pairs={{0,1},{1,2},{2,3},{4,5},{5,6},{6,7},{8,9},{9,10},{10,11},{12,13},{... | collective-permute-start | bytes 4718600 | tf_op jit(solution)/shard_map/ppermute | solution.py:139
  17.8 36.7 %collective-permute-start.5 = (f32[2,512]{1,0:T(2,128)S(1)}, f32[2,512]{1,0:T(2,128)S(1)}, u32[]{:S(2)}, u32[]{:S(2)}) collective-permute-start(f32[2,512]{1,0:T(2,128)S(1)} %get-tuple-element.31), channel_id=1, source_target_pairs={{0,1},{1,2},{2,3},{3,0},{4,5},{5,6},{6,7},{7,4},{8,9},{9,10},{10,1... | collective-permute-start | bytes 12296 | tf_op jit(solution)/shard_map/ppermute | solution.py:135
  18.6 35.9 %collective-permute-start.6 = (f32[2,512]{1,0:T(2,128)S(1)}, f32[2,512]{1,0:T(2,128)S(1)}, u32[]{:S(2)}, u32[]{:S(2)}) collective-permute-start(f32[2,512]{1,0:T(2,128)S(1)} %get-tuple-element.31), channel_id=1, source_target_pairs={{0,2},{1,3},{2,0},{3,1},{4,6},{5,7},{6,4},{7,5},{8,10},{9,11},{10,... | collective-permute-start | bytes 12296 | tf_op jit(solution)/shard_map/ppermute | solution.py:135
  20.8 33.7 %collective-permute-start.7 = (f32[2,512]{1,0:T(2,128)S(1)}, f32[2,512]{1,0:T(2,128)S(1)}, u32[]{:S(2)}, u32[]{:S(2)}) collective-permute-start(f32[2,512]{1,0:T(2,128)S(1)} %get-tuple-element.31), channel_id=1, source_target_pairs={{0,3},{1,0},{2,1},{3,2},{4,7},{5,4},{6,5},{7,6},{8,11},{9,8},{10,9... | collective-permute-start | bytes 12296 | tf_op jit(solution)/shard_map/ppermute | solution.py:135
  47.1 37.7 %collective-permute-start.3 = (bf16[512,1536]{1,0:T(8,128)(2,1)}, bf16[512,1536]{1,0:T(8,128)(2,1)}, u32[]{:S(2)}, u32[]{:S(2)}) collective-permute-start(bf16[512,1536]{1,0:T(8,128)(2,1)} %collective-permute-done.2.refs_1_.refs_0_), channel_id=1, source_target_pairs={{2,1},{1,0},{6,5},{5,4},{10,9},{9,8},{14,13},{13,12},{18,17},{17,1... | collective-permute-start | bytes 4718600 | tf_op jit(solution)/shard_map/ppermute | solution.py:139
  48.4 36.4 %collective-permute-start.1 = (bf16[512,1536]{1,0:T(8,128)(2,1)}, bf16[512,1536]{1,0:T(8,128)(2,1)}, u32[]{:S(2)}, u32[]{:S(2)}) collective-permute-start(bf16[512,1536]{1,0:T(8,128)(2,1)} %collective-permute-done.refs_0_), channel_id=1, source_target_pairs={{1,2},{2,3},{5,6},{6,7},{9,10},{10,11},{13,14},{14,15},{17,18},{18... | collective-permute-start | bytes 4718600 | tf_op jit(solution)/shard_map/ppermute | solution.py:139
  54.5 110.3 %copy-start.12 = (s32[54]{0:T(128)}, s32[54]{0:T(128)S(1)}, u32[]{:S(2)}) copy-start(s32[54]{0:T(128)S(1)} %concatenate.9.facts_ref) | copy-start | bytes 652
  86.4 37.2 %collective-permute-start.4 = (bf16[512,1536]{1,0:T(8,128)(2,1)S(1)}, bf16[512,1536]{1,0:T(8,128)(2,1)S(1)}, u32[]{:S(2)}, u32[]{:S(2)}) collective-permute-start(bf16[512,1536]{1,0:T(8,128)(2,1)S(1)} %broadcast_select_fusion.refs_0_), channel_id=1, source_target_pairs={{2,3},{1,0},{6,7},{5,4},{10,11},{9,8},{14,15},{13,12},{18,19},{17,... | collective-permute-start | bytes 4718600 | tf_op jit(solution)/shard_map/ppermute | solution.py:158
  99.3 25.4 %copy-start.7 = (bf16[96,1536]{1,0:T(8,128)(2,1)S(1)}, bf16[96,1536]{1,0:T(8,128)(2,1)}, u32[]{:S(2)}) copy-start(bf16[96,1536]{1,0:T(8,128)(2,1)} %get-tuple-element.16.refs_11_) | copy-start | bytes 884740
  99.3 25.4 %copy-start.8 = (bf16[96,1536]{1,0:T(8,128)(2,1)S(1)}, bf16[96,1536]{1,0:T(8,128)(2,1)}, u32[]{:S(2)}) copy-start(bf16[96,1536]{1,0:T(8,128)(2,1)} %get-tuple-element.15.refs_10_) | copy-start | bytes 884740
  99.3 25.4 %copy-start.10 = (bf16[96,1536]{1,0:T(8,128)(2,1)S(1)}, bf16[96,1536]{1,0:T(8,128)(2,1)}, u32[]{:S(2)}) copy-start(bf16[96,1536]{1,0:T(8,128)(2,1)} %get-tuple-element.14.refs_9_) | copy-start | bytes 884740
  134.0 47.1 %copy-start.1 = (bf16[288,512]{1,0:T(8,128)(2,1)}, bf16[288,512]{1,0:T(8,128)(2,1)S(1)}, u32[]{:S(2)}) copy-start(bf16[288,512]{1,0:T(8,128)(2,1)S(1)} %get-tuple-element.17.refs_0_) | copy-start | bytes 884740
  134.0 47.1 %copy-start.2 = (bf16[4,288,512]{2,1,0:T(8,128)(2,1)}, bf16[4,288,512]{2,1,0:T(8,128)(2,1)S(1)}, u32[]{:S(2)}) copy-start(bf16[4,288,512]{2,1,0:T(8,128)(2,1)S(1)} %get-tuple-element.18.refs_4_) | copy-start | bytes 3538948
  134.1 47.1 %copy-start.4 = (bf16[288,512]{1,0:T(8,128)(2,1)}, bf16[288,512]{1,0:T(8,128)(2,1)S(1)}, u32[]{:S(2)}) copy-start(bf16[288,512]{1,0:T(8,128)(2,1)S(1)} %get-tuple-element.19.refs_1_) | copy-start | bytes 884740
  134.1 47.1 %copy-start.5 = (bf16[288,512]{1,0:T(8,128)(2,1)}, bf16[288,512]{1,0:T(8,128)(2,1)S(1)}, u32[]{:S(2)}) copy-start(bf16[288,512]{1,0:T(8,128)(2,1)S(1)} %get-tuple-element.20.refs_2_) | copy-start | bytes 884740
  134.1 47.1 %copy-start.6 = (bf16[288,512]{1,0:T(8,128)(2,1)}, bf16[288,512]{1,0:T(8,128)(2,1)S(1)}, u32[]{:S(2)}) copy-start(bf16[288,512]{1,0:T(8,128)(2,1)S(1)} %get-tuple-element.21.refs_3_) | copy-start | bytes 884740
  134.1 30.7 %copy-start.13 = (s32[8,8]{1,0:T(8,128)S(1)}, s32[8,8]{1,0:T(8,128)}, u32[]{:S(2)}) copy-start(s32[8,8]{1,0:T(8,128)} %pair_ref.1) | copy-start | bytes 772
  134.1 3.6 %collective-permute-start.8 = (bf16[4,288,512]{2,1,0:T(8,128)(2,1)S(1)}, bf16[4,288,512]{2,1,0:T(8,128)(2,1)S(1)}, u32[]{:S(2)}, u32[]{:S(2)}) collective-permute-start(bf16[4,288,512]{2,1,0:T(8,128)(2,1)S(1)} %get-tuple-element.18.refs_4_), channel_id=1, source_target_pairs={{0,4},{4,0},{8,12},{12,8},{16,20},{20,16},{24,28},{28,24},{1,5},{5... | collective-permute-start | bytes 3538952 | tf_op jit(solution)/shard_map/ppermute | solution.py:336
  134.2 16.2 %collective-permute-start.11 = (bf16[288,512]{1,0:T(8,128)(2,1)S(1)}, bf16[288,512]{1,0:T(8,128)(2,1)S(1)}, u32[]{:S(2)}, u32[]{:S(2)}) collective-permute-start(bf16[288,512]{1,0:T(8,128)(2,1)S(1)} %get-tuple-element.20.refs_2_), channel_id=1, source_target_pairs={{0,16},{4,20},{8,24},{12,28},{16,0},{20,4},{24,8},{28,12},{1,17},{... | collective-permute-start | bytes 884744 | tf_op jit(solution)/shard_map/ppermute | solution.py:336
  135.8 17.1 %collective-permute-start.13 = (bf16[288,512]{1,0:T(8,128)(2,1)S(1)}, bf16[288,512]{1,0:T(8,128)(2,1)S(1)}, u32[]{:S(2)}, u32[]{:S(2)}) collective-permute-start(bf16[288,512]{1,0:T(8,128)(2,1)S(1)} %get-tuple-element.21.refs_3_), channel_id=1, source_target_pairs={{0,24},{4,28},{8,16},{12,20},{16,8},{20,12},{24,0},{28,4},{1,25},{... | collective-permute-start | bytes 884744 | tf_op jit(solution)/shard_map/ppermute | solution.py:336
  137.2 15.6 %collective-permute-start.9 = (bf16[288,512]{1,0:T(8,128)(2,1)S(1)}, bf16[288,512]{1,0:T(8,128)(2,1)S(1)}, u32[]{:S(2)}, u32[]{:S(2)}) collective-permute-start(bf16[288,512]{1,0:T(8,128)(2,1)S(1)} %get-tuple-element.19.refs_1_), channel_id=1, source_target_pairs={{0,8},{4,12},{8,0},{12,4},{16,24},{20,28},{24,16},{28,20},{1,9},{5... | collective-permute-start | bytes 884744 | tf_op jit(solution)/shard_map/ppermute | solution.py:336
  137.8 20.4 %collective-permute-start.10 = (bf16[288,512]{1,0:T(8,128)(2,1)S(1)}, bf16[288,512]{1,0:T(8,128)(2,1)S(1)}, u32[]{:S(2)}, u32[]{:S(2)}) collective-permute-start(bf16[288,512]{1,0:T(8,128)(2,1)S(1)} %get-tuple-element.28), channel_id=1, source_target_pairs={{0,8},{4,12},{8,0},{12,4},{16,24},{20,28},{24,16},{28,20},{1,9},{5... | collective-permute-start | bytes 884744 | tf_op jit(solution)/shard_map/ppermute | solution.py:336
  139.4 18.9 %collective-permute-start.12 = (bf16[288,512]{1,0:T(8,128)(2,1)S(1)}, bf16[288,512]{1,0:T(8,128)(2,1)S(1)}, u32[]{:S(2)}, u32[]{:S(2)}) collective-permute-start(bf16[288,512]{1,0:T(8,128)(2,1)S(1)} %get-tuple-element.27), channel_id=1, source_target_pairs={{0,16},{4,20},{8,24},{12,28},{16,0},{20,4},{24,8},{28,12},{1,17},{... | collective-permute-start | bytes 884744 | tf_op jit(solution)/shard_map/ppermute | solution.py:336
  150.4 14.4 %collective-permute-start.14 = (bf16[288,512]{1,0:T(8,128)(2,1)S(1)}, bf16[288,512]{1,0:T(8,128)(2,1)S(1)}, u32[]{:S(2)}, u32[]{:S(2)}) collective-permute-start(bf16[288,512]{1,0:T(8,128)(2,1)S(1)} %get-tuple-element.26), channel_id=1, source_target_pairs={{0,24},{4,28},{8,16},{12,20},{16,8},{20,12},{24,0},{28,4},{1,25},{... | collective-permute-start | bytes 884744 | tf_op jit(solution)/shard_map/ppermute | solution.py:336
  164.7 28.1 %copy-start.9 = (bf16[96,1536]{1,0:T(8,128)(2,1)S(1)}, bf16[96,1536]{1,0:T(8,128)(2,1)}, u32[]{:S(2)}) copy-start(bf16[96,1536]{1,0:T(8,128)(2,1)} %get-tuple-element.15.refs_10_) | copy-start | bytes 884740
  181.2 17.6 %copy-start.3 = (bf16[2,96,512]{2,1,0:T(8,128)(2,1)}, bf16[2,96,512]{2,1,0:T(8,128)(2,1)S(1)}, u32[]{:S(2)}) copy-start(bf16[2,96,512]{2,1,0:T(8,128)(2,1)S(1)} %get-tuple-element.22.refs_0_) | copy-start | bytes 589828
  181.2 8.8 %collective-permute-start.17 = (bf16[2,96,512]{2,1,0:T(8,128)(2,1)S(1)}, bf16[2,96,512]{2,1,0:T(8,128)(2,1)S(1)}, u32[]{:S(2)}, u32[]{:S(2)}) collective-permute-start(bf16[2,96,512]{2,1,0:T(8,128)(2,1)S(1)} %get-tuple-element.25), channel_id=1, source_target_pairs={{0,24},{4,28},{8,16},{12,20},{16,8},{20,12},{24,0},{28,4},{1,25},{... | collective-permute-start | bytes 589832 | tf_op jit(solution)/shard_map/ppermute | solution.py:336
  182.7 9.8 %collective-permute-start.16 = (bf16[2,96,512]{2,1,0:T(8,128)(2,1)S(1)}, bf16[2,96,512]{2,1,0:T(8,128)(2,1)S(1)}, u32[]{:S(2)}, u32[]{:S(2)}) collective-permute-start(bf16[2,96,512]{2,1,0:T(8,128)(2,1)S(1)} %get-tuple-element.24), channel_id=1, source_target_pairs={{0,16},{4,20},{8,24},{12,28},{16,0},{20,4},{24,8},{28,12},{1,17},{... | collective-permute-start | bytes 589832 | tf_op jit(solution)/shard_map/ppermute | solution.py:336
  184.3 8.3 %collective-permute-start.15 = (bf16[2,96,512]{2,1,0:T(8,128)(2,1)S(1)}, bf16[2,96,512]{2,1,0:T(8,128)(2,1)S(1)}, u32[]{:S(2)}, u32[]{:S(2)}) collective-permute-start(bf16[2,96,512]{2,1,0:T(8,128)(2,1)S(1)} %get-tuple-element.23), channel_id=1, source_target_pairs={{0,8},{4,12},{8,0},{12,4},{16,24},{20,28},{24,16},{28,20},{1,9},{5... | collective-permute-start | bytes 589832 | tf_op jit(solution)/shard_map/ppermute | solution.py:336
  190.1 8.8 %copy-start.20 = (bf16[2,96,512]{2,1,0:T(8,128)(2,1)}, bf16[2,96,512]{2,1,0:T(8,128)(2,1)S(1)}, u32[]{:S(2)}) copy-start(bf16[2,96,512]{2,1,0:T(8,128)(2,1)S(1)} %collective-permute-done.17.refs_3_) | copy-start | bytes 589828
  192.6 6.3 %copy-start.21 = (bf16[2,96,512]{2,1,0:T(8,128)(2,1)}, bf16[2,96,512]{2,1,0:T(8,128)(2,1)S(1)}, u32[]{:S(2)}) copy-start(bf16[2,96,512]{2,1,0:T(8,128)(2,1)S(1)} %collective-permute-done.16.refs_2_) | copy-start | bytes 589828
  192.7 6.2 %collective-permute-start.18 = (bf16[4,96,512]{2,1,0:T(8,128)(2,1)S(1)}, bf16[4,96,512]{2,1,0:T(8,128)(2,1)S(1)}, u32[]{:S(2)}, u32[]{:S(2)}) collective-permute-start(bf16[4,96,512]{2,1,0:T(8,128)(2,1)S(1)} %pad_maximum_fusion), channel_id=1, source_target_pairs={{0,4},{4,0},{8,12},{12,8},{16,20},{20,16},{24,28},{28,24},{1,5},{5... | collective-permute-start | bytes 1179656 | tf_op jit(solution)/shard_map/ppermute | solution.py:336
  192.8 13.1 %collective-permute-start.24 = (bf16[96,1536]{1,0:T(8,128)(2,1)S(1)}, bf16[96,1536]{1,0:T(8,128)(2,1)S(1)}, u32[]{:S(2)}, u32[]{:S(2)}) collective-permute-start(bf16[96,1536]{1,0:T(8,128)(2,1)S(1)} %copy-done.10), channel_id=1, source_target_pairs={{0,1},{1,2},{2,3},{3,0},{4,5},{5,6},{6,7},{7,4},{8,9},{9,10},{10,1... | collective-permute-start | bytes 884744 | tf_op jit(solution)/shard_map/ppermute | solution.py:135
  192.8 25.4 %collective-permute-start.25 = (bf16[96,1536]{1,0:T(8,128)(2,1)S(1)}, bf16[96,1536]{1,0:T(8,128)(2,1)S(1)}, u32[]{:S(2)}, u32[]{:S(2)}) collective-permute-start(bf16[96,1536]{1,0:T(8,128)(2,1)S(1)} %copy-done.9), channel_id=1, source_target_pairs={{0,2},{1,3},{2,0},{3,1},{4,6},{5,7},{6,4},{7,5},{8,10},{9,11},{10,... | collective-permute-start | bytes 884744 | tf_op jit(solution)/shard_map/ppermute | solution.py:135
  198.4 19.8 %collective-permute-start.26 = (bf16[96,1536]{1,0:T(8,128)(2,1)S(1)}, bf16[96,1536]{1,0:T(8,128)(2,1)S(1)}, u32[]{:S(2)}, u32[]{:S(2)}) collective-permute-start(bf16[96,1536]{1,0:T(8,128)(2,1)S(1)} %copy-done.7), channel_id=1, source_target_pairs={{0,3},{1,0},{2,1},{3,2},{4,7},{5,4},{6,5},{7,6},{8,11},{9,8},{10,9... | collective-permute-start | bytes 884744 | tf_op jit(solution)/shard_map/ppermute | solution.py:135
  205.9 12.3 %copy-start.24 = (bf16[96,1536]{1,0:T(8,128)(2,1)}, bf16[96,1536]{1,0:T(8,128)(2,1)S(1)}, u32[]{:S(2)}) copy-start(bf16[96,1536]{1,0:T(8,128)(2,1)S(1)} %collective-permute-done.24.refs_0_) | copy-start | bytes 884740
  221.3 25.7 %collective-permute-start.19 = (bf16[768,512]{1,0:T(8,128)(2,1)S(1)}, bf16[768,512]{1,0:T(8,128)(2,1)S(1)}, u32[]{:S(2)}, u32[]{:S(2)}) collective-permute-start(bf16[768,512]{1,0:T(8,128)(2,1)S(1)} %bitcast.64), channel_id=1, source_target_pairs={{0,1},{1,2},{2,3},{4,5},{5,6},{6,7},{8,9},{9,10},{10,11},{12,13},{... | collective-permute-start | bytes 2359304 | tf_op jit(solution)/shard_map/ppermute | solution.py:139
  230.0 21.1 %collective-permute-start.21 = (bf16[768,512]{1,0:T(8,128)(2,1)S(1)}, bf16[768,512]{1,0:T(8,128)(2,1)S(1)}, u32[]{:S(2)}, u32[]{:S(2)}) collective-permute-start(bf16[768,512]{1,0:T(8,128)(2,1)S(1)} %bitcast.65), channel_id=1, source_target_pairs={{3,2},{2,1},{1,0},{7,6},{6,5},{5,4},{11,10},{10,9},{9,8},{15,14},{... | collective-permute-start | bytes 2359304 | tf_op jit(solution)/shard_map/ppermute | solution.py:139
  247.0 5.5 %collective-permute-start.20 = (bf16[768,512]{1,0:T(8,128)(2,1)S(1)}, bf16[768,512]{1,0:T(8,128)(2,1)S(1)}, u32[]{:S(2)}, u32[]{:S(2)}) collective-permute-start(bf16[768,512]{1,0:T(8,128)(2,1)S(1)} %collective-permute-done.19.refs_1_), channel_id=1, source_target_pairs={{1,2},{2,3},{5,6},{6,7},{9,10},{10,11},{13,14},{14,15},{17,18},{18... | collective-permute-start | bytes 2359304 | tf_op jit(solution)/shard_map/ppermute | solution.py:139
  251.1 20.2 %collective-permute-start.22 = (bf16[768,512]{1,0:T(8,128)(2,1)S(1)}, bf16[768,512]{1,0:T(8,128)(2,1)S(1)}, u32[]{:S(2)}, u32[]{:S(2)}) collective-permute-start(bf16[768,512]{1,0:T(8,128)(2,1)S(1)} %collective-permute-done.21.refs_2_.refs_3_), channel_id=1, source_target_pairs={{2,1},{1,0},{6,5},{5,4},{10,9},{9,8},{14,13},{13,12},{18,17},{17,1... | collective-permute-start | bytes 2359304 | tf_op jit(solution)/shard_map/ppermute | solution.py:139
  252.5 23.8 %copy-start.17 = (bf16[768,512]{1,0:T(8,128)(2,1)}, bf16[768,512]{1,0:T(8,128)(2,1)S(1)}, u32[]{:S(2)}) copy-start(bf16[768,512]{1,0:T(8,128)(2,1)S(1)} %collective-permute-done.20.refs_5_) | copy-start | bytes 2359300
  271.4 19.4 %collective-permute-start.23 = (bf16[768,512]{1,0:T(8,128)(2,1)S(1)}, bf16[768,512]{1,0:T(8,128)(2,1)S(1)}, u32[]{:S(2)}, u32[]{:S(2)}) collective-permute-start(bf16[768,512]{1,0:T(8,128)(2,1)S(1)} %broadcast_select_fusion.1.refs_0_), channel_id=1, source_target_pairs={{2,3},{1,0},{6,7},{5,4},{10,11},{9,8},{14,15},{13,12},{18,19},{17,... | collective-permute-start | bytes 2359304 | tf_op jit(solution)/shard_map/ppermute | solution.py:158
  (12 other events, 33.0 us)
Sparse Core Ops, SparseCore 0:
  221.4 52.4 all-gather.2

commit v3 on v1

--- a/solution.py
+++ b/solution.py
@@ -197,7 +197,9 @@
         for head in range(turned_ref.shape[0]):
             part = turned[head * HD : head * HD + ROT]
             swapped = jnp.concatenate([part[half:], part[:half]], axis=0)
-            turned_ref[head, :ROT] = (part * cos_ref[...] + swapped * sin_ref[...]).astype(jnp.bfloat16)
+            rotated = part * cos_ref[...] + swapped * sin_ref[...]
+            rest = turned[head * HD + ROT : head * HD + 32]
+            turned_ref[head, :32] = jnp.concatenate([rotated, rest], axis=0).astype(jnp.bfloat16)
 
     for distance in range(4):
         head = 2 * (chip ^ distance)

time: 283 us -> 283 us (level)
  no operation moved by 1% of the time
where the time goes in v3:
time: 283 us; the launch traced here: 282 us
  waiting for transfers between devices  121 us (43%)
  Pallas kernels  85.7 us (30%)
  starting transfers between devices  49.4 us (17%)
  between operations  14.8 us (5%)
  local copies, waits for them, and re-layouts  5.96 us (2%)
  other arithmetic  5.38 us (2%)
    ppermute x8, waiting for transfers between devices, line_hop(): return (lax.ppermute(up, 'tp', ups), lax.ppermute(down, 'tp', downs))  84.5 us
    pallas_call x4, Pallas kernels, project(): pl.pallas_call(functools.partial(project_kernel, step, len(shards)), grid...  41.7 us
    ppermute x11, waiting for transfers between devices, swap(): lax.ppermute(value, 'blk', [(place, place ^ distance) for place in range(...  20.4 us
    ppermute x8, starting transfers between devices, line_hop(): return (lax.ppermute(up, 'tp', ups), lax.ppermute(down, 'tp', downs))  17.2 us
    pallas_call x2, Pallas kernels, combine(): pl.pallas_call(functools.partial(combine_kernel, steps, tuple((len(step)...  16.9 us
    pallas_call x1, Pallas kernels, attend(): pl.pallas_call(attend_kernel, in_specs=[smem, smem, vmem] + [vmem] * len(...  16.4 us
    ppermute x6, starting transfers between devices, turn(): lax.ppermute(value, 'tp', [(source, (source + distance) % 4) for source i...  16.4 us
    ppermute x2, waiting for transfers between devices, gather_line(): outer = lax.ppermute(inner, 'tp', [(2, 3), (1, 0)])  15.9 us
  transfers between devices with their start and end apart: 28, of which 12 were waited for; matrix products, arithmetic and copies ran while one was open for 2% of the time, Pallas kernels for 24%

profile of v3, /device:TPU:0, one launch (start us, length us, event | category | flops | bytes accessed | tf_op | source)
XLA Modules:
  0.0 282.1 jit_solution(17475618441352092989)
XLA Ops:
  7.2 1.4 collective-permute-start.2
  8.7 6.8 %collective-permute-start = (bf16[512,1536]{1,0:T(8,128)(2,1)}, bf16[512,1536]{1,0:T(8,128)(2,1)}, u32[]{:S(2)}, u32[]{:S(2)}) collective-permute-start(bf16[512,1536]{1,0:T(8,128)(2,1)} %refs_0_.1), channel_id=1, source_target_pairs={{0,1},{1,2},{2,3},{4,5},{5,6},{6,7},{8,9},{9,10},{10,11},{12,13},{... | collective-permute-start | bytes 4718600 | tf_op jit(solution)/shard_map/ppermute | solution.py:139
  15.5 1.7 convert_reduce_fusion
  17.7 0.9 collective-permute-start.5
  18.6 2.2 collective-permute-start.6
  20.8 2.8 %collective-permute-start.7 = (f32[2,512]{1,0:T(2,128)S(1)}, f32[2,512]{1,0:T(2,128)S(1)}, u32[]{:S(2)}, u32[]{:S(2)}) collective-permute-start(f32[2,512]{1,0:T(2,128)S(1)} %get-tuple-element.31), channel_id=1, source_target_pairs={{0,3},{1,0},{2,1},{3,2},{4,7},{5,4},{6,5},{7,6},{8,11},{9,8},{10,9... | collective-permute-start | bytes 12296 | tf_op jit(solution)/shard_map/ppermute | solution.py:135
  24.3 22.8 %collective-permute-done.2.refs_1_.refs_0_ = bf16[512,1536]{1,0:T(8,128)(2,1)} collective-permute-done((bf16[512,1536]{1,0:T(8,128)(2,1)}, bf16[512,1536]{1,0:T(8,128)(2,1)}, u32[]{:S(2)}, u32[]{:S(2)}) %collective-permute-start.2) | collective-permute-done | bytes 1572896 | tf_op jit(solution)/shard_map/ppermute | solution.py:139
  47.1 1.3 collective-permute-start.3
  48.4 1.8 collective-permute-start.1
  51.5 2.9 %shares.1 = (bf16[96,1536]{1,0:T(8,128)(2,1)}, bf16[96,1536]{1,0:T(8,128)(2,1)}, bf16[96,1536]{1,0:T(8,128)(2,1)}) custom-call(s32[4]{0:T(128)} %pad_add_fusion.facts_ref, bf16[768,6144]{1,0:T(8,128)(2,1)} %refs_6_.1), custom_call_target="tpu_custom_call" | custom-call | bytes 2097152 | tf_op jit(solution)/shard_map/shares/pallas_call | solution.py:463
  55.0 9.0 %project.4.refs_6_ = f32[3,512,768]{2,1,0:T(8,128)} custom-call(s32[54]{0:T(128)S(1)} %concatenate.9.facts_ref, bf16[512,1536]{1,0:T(8,128)(2,1)S(1)} %copy-done, f32[512,1]{1,0:T(8,128)S(1)} %copy.42.refs_1_.refs_2_.refs_3_, f32[512,1]{1,0:T(8,128)S(1)} %copy.43.refs_2_.refs_3_.refs_4_, f32[4,1,1536]{2,1,0:T(1,128)S(1)} %bitcast.50, ...), custom_call_target="tpu_custom_call" | custom-call | flops 603979776 | tf_op jit(solution)/shard_map/project/pallas_call | solution.py:234
  64.1 20.7 %collective-permute-done.3.refs_1_ = bf16[512,1536]{1,0:T(8,128)(2,1)} collective-permute-done((bf16[512,1536]{1,0:T(8,128)(2,1)}, bf16[512,1536]{1,0:T(8,128)(2,1)}, u32[]{:S(2)}, u32[]{:S(2)}) %collective-permute-start.3) | collective-permute-done | bytes 1572896 | tf_op jit(solution)/shard_map/ppermute | solution.py:139
  84.8 1.6 broadcast_select_fusion.refs_0_
  86.4 1.5 collective-permute-start.4
  87.9 11.4 %project.5.refs_7_ = f32[3,512,768]{2,1,0:T(8,128)} custom-call(s32[54]{0:T(128)S(1)} %concatenate.9.facts_ref, bf16[512,1536]{1,0:T(8,128)(2,1)} %collective-permute-done.refs_0_, bf16[512,1536]{1,0:T(8,128)(2,1)} %collective-permute-done.2.refs_1_.refs_0_, f32[512,1]{1,0:T(8,128)S(1)} %copy.42.refs_1_.refs_2_.refs_3_, ...), custom_call_target="tpu_custom_call" | custom-call | flops 12079595520 | tf_op jit(solution)/shard_map/project/pallas_call | solution.py:234
  99.3 11.9 %project.6.refs_6_ = f32[3,512,768]{2,1,0:T(8,128)} custom-call(s32[54]{0:T(128)S(1)} %concatenate.9.facts_ref, bf16[512,1536]{1,0:T(8,128)(2,1)} %collective-permute-done.2.refs_1_.refs_0_, bf16[512,1536]{1,0:T(8,128)(2,1)} %collective-permute-done.3.refs_1_, bf16[512,1536]{1,0:T(8,128)(2,1)} %collective-permute-done.1.refs_2_, ...), custom_call_target="tpu_custom_call" | custom-call | flops 12079595520 | tf_op jit(solution)/shard_map/project/pallas_call | solution.py:234
  111.2 12.3 %collective-permute-done.4.refs_1_ = bf16[512,1536]{1,0:T(8,128)(2,1)S(1)} collective-permute-done((bf16[512,1536]{1,0:T(8,128)(2,1)S(1)}, bf16[512,1536]{1,0:T(8,128)(2,1)S(1)}, u32[]{:S(2)}, u32[]{:S(2)}) %collective-permute-start.4) | collective-permute-done | bytes 1572896 | tf_op jit(solution)/shard_map/ppermute | solution.py:158
  123.5 1.1 copy-done.15
  124.7 9.3 %project.7 = (bf16[288,512]{1,0:T(8,128)(2,1)S(1)}, bf16[288,512]{1,0:T(8,128)(2,1)S(1)}, bf16[288,512]{1,0:T(8,128)(2,1)S(1)}, bf16[288,512]{1,0:T(8,128)(2,1)S(1)}, bf16[4,288,512]{2,1,0:T(8,128)(2,1)S(1)}) custom-call(s32[54]{0:T(128)S(1)} %concatenate.9.facts_ref, bf16[512,1536]{1,0:T(8,128)(2,1)S(1)} %broadcast_select_fusion.refs_0_, ...), custom_call_target="tpu_custom_call" | custom-call | flops 3623878656 | tf_op jit(solution)/shard_map/project/pallas_call | solution.py:234
  134.2 1.6 collective-permute-start.11
  135.8 1.4 collective-permute-start.13
  137.8 1.6 collective-permute-start.10
  139.4 1.5 collective-permute-start.12
  140.9 9.5 %collective-permute-done.11.refs_4_ = bf16[288,512]{1,0:T(8,128)(2,1)S(1)} collective-permute-done((bf16[288,512]{1,0:T(8,128)(2,1)S(1)}, bf16[288,512]{1,0:T(8,128)(2,1)S(1)}, u32[]{:S(2)}, u32[]{:S(2)}) %collective-permute-start.11) | collective-permute-done | bytes 294944 | tf_op jit(solution)/shard_map/ppermute | solution.py:338
  150.4 2.4 collective-permute-start.14
  152.8 5.6 %collective-permute-start.25 = (bf16[96,1536]{1,0:T(8,128)(2,1)S(1)}, bf16[96,1536]{1,0:T(8,128)(2,1)S(1)}, u32[]{:S(2)}, u32[]{:S(2)}) collective-permute-start(bf16[96,1536]{1,0:T(8,128)(2,1)S(1)} %copy-done.9), channel_id=1, source_target_pairs={{0,2},{1,3},{2,0},{3,1},{4,6},{5,7},{6,4},{7,5},{8,10},{9,11},{10,... | collective-permute-start | bytes 884744 | tf_op jit(solution)/shard_map/ppermute | solution.py:135
  158.4 4.9 %collective-permute-start.26 = (bf16[96,1536]{1,0:T(8,128)(2,1)S(1)}, bf16[96,1536]{1,0:T(8,128)(2,1)S(1)}, u32[]{:S(2)}, u32[]{:S(2)}) collective-permute-start(bf16[96,1536]{1,0:T(8,128)(2,1)S(1)} %copy-done.8), channel_id=1, source_target_pairs={{0,3},{1,0},{2,1},{3,2},{4,7},{5,4},{6,5},{7,6},{8,11},{9,8},{10,9... | collective-permute-start | bytes 884744 | tf_op jit(solution)/shard_map/ppermute | solution.py:135
  163.3 1.5 collective-permute-done.14.refs_7_
  164.8 16.4 %attend.1 = (bf16[2,96,512]{2,1,0:T(8,128)(2,1)S(1)}, bf16[2,96,512]{2,1,0:T(8,128)(2,1)S(1)}, bf16[2,96,512]{2,1,0:T(8,128)(2,1)S(1)}, bf16[2,96,512]{2,1,0:T(8,128)(2,1)S(1)}) custom-call(s32[54]{0:T(128)S(1)} %concatenate.9.facts_ref, s32[8,8]{1,0:T(8,128)S(1)} %copy-done.13, s32[8,1,512]{2,1,0:T(1,128)S(1)} %bitcast.55, ...), custom_call_target="tpu_custom_call" | custom-call | flops 1000 | bytes 1000 | tf_op jit(solution)/shard_map/attend/pallas_call | solution.py:317
  183.5 2.2 stack.114
  185.6 1.5 collective-permute-start.17
  187.1 1.5 collective-permute-start.16
  189.2 5.3 %collective-permute-done.17.refs_3_ = bf16[2,96,512]{2,1,0:T(8,128)(2,1)S(1)} collective-permute-done((bf16[2,96,512]{2,1,0:T(8,128)(2,1)S(1)}, bf16[2,96,512]{2,1,0:T(8,128)(2,1)S(1)}, u32[]{:S(2)}, u32[]{:S(2)}) %collective-permute-start.17) | collective-permute-done | bytes 196640 | tf_op jit(solution)/shard_map/ppermute | solution.py:338
  194.5 2.5 collective-permute-done.16.refs_2_
  197.2 1.7 collective-permute-done.18.refs_4_
  199.6 2.3 order.1
  201.9 2.7 collective-permute-start.19
  204.6 1.3 collective-permute-start.21
  205.9 16.0 %collective-permute-done.19.refs_1_ = bf16[768,512]{1,0:T(8,128)(2,1)S(1)} collective-permute-done((bf16[768,512]{1,0:T(8,128)(2,1)}, bf16[768,512]{1,0:T(8,128)(2,1)S(1)}, u32[]{:S(2)}, u32[]{:S(2)}) %collective-permute-start.19) | collective-permute-done | bytes 786464 | tf_op jit(solution)/shard_map/ppermute | solution.py:139
  222.6 4.5 %collective-permute-done.21.refs_2_.refs_3_ = bf16[768,512]{1,0:T(8,128)(2,1)S(1)} collective-permute-done((bf16[768,512]{1,0:T(8,128)(2,1)}, bf16[768,512]{1,0:T(8,128)(2,1)S(1)}, u32[]{:S(2)}, u32[]{:S(2)}) %collective-permute-start.21) | collective-permute-done | bytes 786464 | tf_op jit(solution)/shard_map/ppermute | solution.py:139
  227.2 1.3 collective-permute-start.22
  228.5 20.4 %collective-permute-done.22.refs_4_ = bf16[768,512]{1,0:T(8,128)(2,1)S(1)} collective-permute-done((bf16[768,512]{1,0:T(8,128)(2,1)S(1)}, bf16[768,512]{1,0:T(8,128)(2,1)S(1)}, u32[]{:S(2)}, u32[]{:S(2)}) %collective-permute-start.22) | collective-permute-done | bytes 786464 | tf_op jit(solution)/shard_map/ppermute | solution.py:139
  249.0 1.5 collective-permute-start.23
  250.5 3.3 %pages.1 = bf16[2,32,16,768]{3,2,1,0:T(8,128)(2,1)} custom-call(s32[54]{0:T(128)} %copy-done.12, bf16[288,512]{1,0:T(8,128)(2,1)} %copy-done.3, bf16[288,512]{1,0:T(8,128)(2,1)} %copy-done.5, bf16[288,512]{1,0:T(8,128)(2,1)} %copy-done.6, bf16[288,512]{1,0:T(8,128)(2,1)} %copy-done.7, bf16[4,288,512]{2,1,0:T(8,128)(2,1)} %copy-done.4), custom_call_target="tpu_custom_call" | custom-call | bytes 10485760 | tf_op jit(solution)/shard_map/pages/pallas_call | solution.py:512
  253.9 11.7 %combine.2.refs_3_ = bf16[512,1536]{1,0:T(8,128)(2,1)} custom-call(s32[54]{0:T(128)} %copy-done.12, bf16[768,512]{1,0:T(8,128)(2,1)} %bitcast.64, bf16[768,512]{1,0:T(8,128)(2,1)} %copy-done.28, bf16[768,512]{1,0:T(8,128)(2,1)} %copy-done.29, bf16[768,512]{1,0:T(8,128)(2,1)} %copy-done.29, bf16[768,512]{1,0:T(8,128)(2,1)} %copy-done.17, ...), custom_call_target="tpu_custom_call" | custom-call | flops 7247757312 | bytes 7077888 | tf_op jit(solution)/shard_map/combine/pallas_call | solution.py:426
  265.6 3.5 %collective-permute-done.23.refs_1_ = bf16[768,512]{1,0:T(8,128)(2,1)S(1)} collective-permute-done((bf16[768,512]{1,0:T(8,128)(2,1)S(1)}, bf16[768,512]{1,0:T(8,128)(2,1)S(1)}, u32[]{:S(2)}, u32[]{:S(2)}) %collective-permute-start.23) | collective-permute-done | bytes 786464 | tf_op jit(solution)/shard_map/ppermute | solution.py:158
  269.1 0.9 copy-done.18
  270.0 5.2 %combine.3 = bf16[512,1536]{1,0:T(8,128)(2,1)} custom-call(s32[54]{0:T(128)} %copy-done.12, bf16[768,512]{1,0:T(8,128)(2,1)} %copy-done.14, bf16[768,512]{1,0:T(8,128)(2,1)} %copy-done.18, bf16[8,3,96,1536]{3,2,1,0:T(8,128)(2,1)} %bitcast.61, bf16[512,1536]{1,0:T(8,128)(2,1)} %combine.2.refs_3_), custom_call_target="tpu_custom_call" | custom-call | flops 2415919104 | bytes 2359296 | tf_op jit(solution)/shard_map/combine/pallas_call | solution.py:426
  (120 shorter events, 8.1 us)
Async XLA Ops:
  7.2 10.0 %copy-start = (bf16[512,1536]{1,0:T(8,128)(2,1)S(1)}, bf16[512,1536]{1,0:T(8,128)(2,1)}, u32[]{:S(2)}) copy-start(bf16[512,1536]{1,0:T(8,128)(2,1)} %refs_0_.1) | copy-start | bytes 4718596
  7.2 16.5 %copy-start.27 = (s32[32]{0:T(128)S(1)}, s32[32]{0:T(128)}, u32[]{:S(2)}) copy-start(s32[32]{0:T(128)} %param.12) | copy-start | bytes 388
  7.2 16.8 %copy-start.26 = (s32[512]{0:T(512)S(1)}, s32[512]{0:T(512)}, u32[]{:S(2)}) copy-start(s32[512]{0:T(512)} %param.13) | copy-start | bytes 6148
  7.2 44.2 %copy-start.30 = (s32[32]{0:T(128)S(1)}, s32[32]{0:T(128)}, u32[]{:S(2)}) copy-start(s32[32]{0:T(128)} %param.15) | copy-start | bytes 388
  7.2 246.7 %all-gather.3.cloned.1.call-start = ((), (), s32[]{:S(2)}) async-start(), calls=%async_computation | async-start | bytes 7962624 | tf_op jit(solution)/shard_map/all_gather | solution.py:583
  7.2 39.8 %collective-permute-start.2 = (bf16[512,1536]{1,0:T(8,128)(2,1)}, bf16[512,1536]{1,0:T(8,128)(2,1)}, u32[]{:S(2)}, u32[]{:S(2)}) collective-permute-start(bf16[512,1536]{1,0:T(8,128)(2,1)} %refs_0_.1), channel_id=1, source_target_pairs={{3,2},{2,1},{1,0},{7,6},{6,5},{5,4},{11,10},{10,9},{9,8},{15,14},{... | collective-permute-start | bytes 4718600 | tf_op jit(solution)/shard_map/ppermute | solution.py:139
  8.7 39.7 %collective-permute-start = (bf16[512,1536]{1,0:T(8,128)(2,1)}, bf16[512,1536]{1,0:T(8,128)(2,1)}, u32[]{:S(2)}, u32[]{:S(2)}) collective-permute-start(bf16[512,1536]{1,0:T(8,128)(2,1)} %refs_0_.1), channel_id=1, source_target_pairs={{0,1},{1,2},{2,3},{4,5},{5,6},{6,7},{8,9},{9,10},{10,11},{12,13},{... | collective-permute-start | bytes 4718600 | tf_op jit(solution)/shard_map/ppermute | solution.py:139
  17.7 36.8 %collective-permute-start.5 = (f32[2,512]{1,0:T(2,128)S(1)}, f32[2,512]{1,0:T(2,128)S(1)}, u32[]{:S(2)}, u32[]{:S(2)}) collective-permute-start(f32[2,512]{1,0:T(2,128)S(1)} %get-tuple-element.31), channel_id=1, source_target_pairs={{0,1},{1,2},{2,3},{3,0},{4,5},{5,6},{6,7},{7,4},{8,9},{9,10},{10,1... | collective-permute-start | bytes 12296 | tf_op jit(solution)/shard_map/ppermute | solution.py:135
  18.6 35.9 %collective-permute-start.6 = (f32[2,512]{1,0:T(2,128)S(1)}, f32[2,512]{1,0:T(2,128)S(1)}, u32[]{:S(2)}, u32[]{:S(2)}) collective-permute-start(f32[2,512]{1,0:T(2,128)S(1)} %get-tuple-element.31), channel_id=1, source_target_pairs={{0,2},{1,3},{2,0},{3,1},{4,6},{5,7},{6,4},{7,5},{8,10},{9,11},{10,... | collective-permute-start | bytes 12296 | tf_op jit(solution)/shard_map/ppermute | solution.py:135
  20.8 33.8 %collective-permute-start.7 = (f32[2,512]{1,0:T(2,128)S(1)}, f32[2,512]{1,0:T(2,128)S(1)}, u32[]{:S(2)}, u32[]{:S(2)}) collective-permute-start(f32[2,512]{1,0:T(2,128)S(1)} %get-tuple-element.31), channel_id=1, source_target_pairs={{0,3},{1,0},{2,1},{3,2},{4,7},{5,4},{6,5},{7,6},{8,11},{9,8},{10,9... | collective-permute-start | bytes 12296 | tf_op jit(solution)/shard_map/ppermute | solution.py:135
  47.1 37.7 %collective-permute-start.3 = (bf16[512,1536]{1,0:T(8,128)(2,1)}, bf16[512,1536]{1,0:T(8,128)(2,1)}, u32[]{:S(2)}, u32[]{:S(2)}) collective-permute-start(bf16[512,1536]{1,0:T(8,128)(2,1)} %collective-permute-done.2.refs_1_.refs_0_), channel_id=1, source_target_pairs={{2,1},{1,0},{6,5},{5,4},{10,9},{9,8},{14,13},{13,12},{18,17},{17,1... | collective-permute-start | bytes 4718600 | tf_op jit(solution)/shard_map/ppermute | solution.py:139
  48.4 36.4 %collective-permute-start.1 = (bf16[512,1536]{1,0:T(8,128)(2,1)}, bf16[512,1536]{1,0:T(8,128)(2,1)}, u32[]{:S(2)}, u32[]{:S(2)}) collective-permute-start(bf16[512,1536]{1,0:T(8,128)(2,1)} %collective-permute-done.refs_0_), channel_id=1, source_target_pairs={{1,2},{2,3},{5,6},{6,7},{9,10},{10,11},{13,14},{14,15},{17,18},{18... | collective-permute-start | bytes 4718600 | tf_op jit(solution)/shard_map/ppermute | solution.py:139
  54.5 110.2 %copy-start.12 = (s32[54]{0:T(128)}, s32[54]{0:T(128)S(1)}, u32[]{:S(2)}) copy-start(s32[54]{0:T(128)S(1)} %concatenate.9.facts_ref) | copy-start | bytes 652
  86.4 37.2 %collective-permute-start.4 = (bf16[512,1536]{1,0:T(8,128)(2,1)S(1)}, bf16[512,1536]{1,0:T(8,128)(2,1)S(1)}, u32[]{:S(2)}, u32[]{:S(2)}) collective-permute-start(bf16[512,1536]{1,0:T(8,128)(2,1)S(1)} %broadcast_select_fusion.refs_0_), channel_id=1, source_target_pairs={{2,3},{1,0},{6,7},{5,4},{10,11},{9,8},{14,15},{13,12},{18,19},{17,... | collective-permute-start | bytes 4718600 | tf_op jit(solution)/shard_map/ppermute | solution.py:158
  99.3 25.4 %copy-start.8 = (bf16[96,1536]{1,0:T(8,128)(2,1)S(1)}, bf16[96,1536]{1,0:T(8,128)(2,1)}, u32[]{:S(2)}) copy-start(bf16[96,1536]{1,0:T(8,128)(2,1)} %get-tuple-element.16.refs_11_) | copy-start | bytes 884740
  99.3 25.4 %copy-start.9 = (bf16[96,1536]{1,0:T(8,128)(2,1)S(1)}, bf16[96,1536]{1,0:T(8,128)(2,1)}, u32[]{:S(2)}) copy-start(bf16[96,1536]{1,0:T(8,128)(2,1)} %get-tuple-element.15.refs_10_) | copy-start | bytes 884740
  99.3 25.4 %copy-start.10 = (bf16[96,1536]{1,0:T(8,128)(2,1)S(1)}, bf16[96,1536]{1,0:T(8,128)(2,1)}, u32[]{:S(2)}) copy-start(bf16[96,1536]{1,0:T(8,128)(2,1)} %get-tuple-element.14.refs_9_) | copy-start | bytes 884740
  134.0 47.1 %copy-start.3 = (bf16[288,512]{1,0:T(8,128)(2,1)}, bf16[288,512]{1,0:T(8,128)(2,1)S(1)}, u32[]{:S(2)}) copy-start(bf16[288,512]{1,0:T(8,128)(2,1)S(1)} %get-tuple-element.17.refs_0_) | copy-start | bytes 884740
  134.0 47.1 %copy-start.4 = (bf16[4,288,512]{2,1,0:T(8,128)(2,1)}, bf16[4,288,512]{2,1,0:T(8,128)(2,1)S(1)}, u32[]{:S(2)}) copy-start(bf16[4,288,512]{2,1,0:T(8,128)(2,1)S(1)} %get-tuple-element.18.refs_4_) | copy-start | bytes 3538948
  134.1 47.1 %copy-start.5 = (bf16[288,512]{1,0:T(8,128)(2,1)}, bf16[288,512]{1,0:T(8,128)(2,1)S(1)}, u32[]{:S(2)}) copy-start(bf16[288,512]{1,0:T(8,128)(2,1)S(1)} %get-tuple-element.19.refs_1_) | copy-start | bytes 884740
  134.1 47.1 %copy-start.6 = (bf16[288,512]{1,0:T(8,128)(2,1)}, bf16[288,512]{1,0:T(8,128)(2,1)S(1)}, u32[]{:S(2)}) copy-start(bf16[288,512]{1,0:T(8,128)(2,1)S(1)} %get-tuple-element.20.refs_2_) | copy-start | bytes 884740
  134.1 47.1 %copy-start.7 = (bf16[288,512]{1,0:T(8,128)(2,1)}, bf16[288,512]{1,0:T(8,128)(2,1)S(1)}, u32[]{:S(2)}) copy-start(bf16[288,512]{1,0:T(8,128)(2,1)S(1)} %get-tuple-element.21.refs_3_) | copy-start | bytes 884740
  134.1 30.7 %copy-start.13 = (s32[8,8]{1,0:T(8,128)S(1)}, s32[8,8]{1,0:T(8,128)}, u32[]{:S(2)}) copy-start(s32[8,8]{1,0:T(8,128)} %pair_ref.1) | copy-start | bytes 772
  134.1 3.6 %collective-permute-start.8 = (bf16[4,288,512]{2,1,0:T(8,128)(2,1)S(1)}, bf16[4,288,512]{2,1,0:T(8,128)(2,1)S(1)}, u32[]{:S(2)}, u32[]{:S(2)}) collective-permute-start(bf16[4,288,512]{2,1,0:T(8,128)(2,1)S(1)} %get-tuple-element.18.refs_4_), channel_id=1, source_target_pairs={{0,4},{4,0},{8,12},{12,8},{16,20},{20,16},{24,28},{28,24},{1,5},{5... | collective-permute-start | bytes 3538952 | tf_op jit(solution)/shard_map/ppermute | solution.py:338
  134.2 16.2 %collective-permute-start.11 = (bf16[288,512]{1,0:T(8,128)(2,1)S(1)}, bf16[288,512]{1,0:T(8,128)(2,1)S(1)}, u32[]{:S(2)}, u32[]{:S(2)}) collective-permute-start(bf16[288,512]{1,0:T(8,128)(2,1)S(1)} %get-tuple-element.20.refs_2_), channel_id=1, source_target_pairs={{0,16},{4,20},{8,24},{12,28},{16,0},{20,4},{24,8},{28,12},{1,17},{... | collective-permute-start | bytes 884744 | tf_op jit(solution)/shard_map/ppermute | solution.py:338
  135.8 17.1 %collective-permute-start.13 = (bf16[288,512]{1,0:T(8,128)(2,1)S(1)}, bf16[288,512]{1,0:T(8,128)(2,1)S(1)}, u32[]{:S(2)}, u32[]{:S(2)}) collective-permute-start(bf16[288,512]{1,0:T(8,128)(2,1)S(1)} %get-tuple-element.21.refs_3_), channel_id=1, source_target_pairs={{0,24},{4,28},{8,16},{12,20},{16,8},{20,12},{24,0},{28,4},{1,25},{... | collective-permute-start | bytes 884744 | tf_op jit(solution)/shard_map/ppermute | solution.py:338
  137.2 15.6 %collective-permute-start.9 = (bf16[288,512]{1,0:T(8,128)(2,1)S(1)}, bf16[288,512]{1,0:T(8,128)(2,1)S(1)}, u32[]{:S(2)}, u32[]{:S(2)}) collective-permute-start(bf16[288,512]{1,0:T(8,128)(2,1)S(1)} %get-tuple-element.19.refs_1_), channel_id=1, source_target_pairs={{0,8},{4,12},{8,0},{12,4},{16,24},{20,28},{24,16},{28,20},{1,9},{5... | collective-permute-start | bytes 884744 | tf_op jit(solution)/shard_map/ppermute | solution.py:338
  137.8 20.6 %collective-permute-start.10 = (bf16[288,512]{1,0:T(8,128)(2,1)S(1)}, bf16[288,512]{1,0:T(8,128)(2,1)S(1)}, u32[]{:S(2)}, u32[]{:S(2)}) collective-permute-start(bf16[288,512]{1,0:T(8,128)(2,1)S(1)} %get-tuple-element.28), channel_id=1, source_target_pairs={{0,8},{4,12},{8,0},{12,4},{16,24},{20,28},{24,16},{28,20},{1,9},{5... | collective-permute-start | bytes 884744 | tf_op jit(solution)/shard_map/ppermute | solution.py:338
  139.4 23.9 %collective-permute-start.12 = (bf16[288,512]{1,0:T(8,128)(2,1)S(1)}, bf16[288,512]{1,0:T(8,128)(2,1)S(1)}, u32[]{:S(2)}, u32[]{:S(2)}) collective-permute-start(bf16[288,512]{1,0:T(8,128)(2,1)S(1)} %get-tuple-element.27), channel_id=1, source_target_pairs={{0,16},{4,20},{8,24},{12,28},{16,0},{20,4},{24,8},{28,12},{1,17},{... | collective-permute-start | bytes 884744 | tf_op jit(solution)/shard_map/ppermute | solution.py:338
  150.4 14.4 %collective-permute-start.14 = (bf16[288,512]{1,0:T(8,128)(2,1)S(1)}, bf16[288,512]{1,0:T(8,128)(2,1)S(1)}, u32[]{:S(2)}, u32[]{:S(2)}) collective-permute-start(bf16[288,512]{1,0:T(8,128)(2,1)S(1)} %get-tuple-element.26), channel_id=1, source_target_pairs={{0,24},{4,28},{8,16},{12,20},{16,8},{20,12},{24,0},{28,4},{1,25},{... | collective-permute-start | bytes 884744 | tf_op jit(solution)/shard_map/ppermute | solution.py:338
  152.8 29.1 %collective-permute-start.24 = (bf16[96,1536]{1,0:T(8,128)(2,1)S(1)}, bf16[96,1536]{1,0:T(8,128)(2,1)S(1)}, u32[]{:S(2)}, u32[]{:S(2)}) collective-permute-start(bf16[96,1536]{1,0:T(8,128)(2,1)S(1)} %copy-done.10), channel_id=1, source_target_pairs={{0,1},{1,2},{2,3},{3,0},{4,5},{5,6},{6,7},{7,4},{8,9},{9,10},{10,1... | collective-permute-start | bytes 884744 | tf_op jit(solution)/shard_map/ppermute | solution.py:135
  152.8 29.1 %collective-permute-start.25 = (bf16[96,1536]{1,0:T(8,128)(2,1)S(1)}, bf16[96,1536]{1,0:T(8,128)(2,1)S(1)}, u32[]{:S(2)}, u32[]{:S(2)}) collective-permute-start(bf16[96,1536]{1,0:T(8,128)(2,1)S(1)} %copy-done.9), channel_id=1, source_target_pairs={{0,2},{1,3},{2,0},{3,1},{4,6},{5,7},{6,4},{7,5},{8,10},{9,11},{10,... | collective-permute-start | bytes 884744 | tf_op jit(solution)/shard_map/ppermute | solution.py:135
  158.4 23.5 %collective-permute-start.26 = (bf16[96,1536]{1,0:T(8,128)(2,1)S(1)}, bf16[96,1536]{1,0:T(8,128)(2,1)S(1)}, u32[]{:S(2)}, u32[]{:S(2)}) collective-permute-start(bf16[96,1536]{1,0:T(8,128)(2,1)S(1)} %copy-done.8), channel_id=1, source_target_pairs={{0,3},{1,0},{2,1},{3,2},{4,7},{5,4},{6,5},{7,6},{8,11},{9,8},{10,9... | collective-permute-start | bytes 884744 | tf_op jit(solution)/shard_map/ppermute | solution.py:135
  181.9 7.3 %copy-start.2 = (bf16[2,96,512]{2,1,0:T(8,128)(2,1)S(1)}, bf16[2,96,512]{2,1,0:T(8,128)(2,1)}, u32[]{:S(2)}) copy-start(bf16[2,96,512]{2,1,0:T(8,128)(2,1)} %copy-done.1) | copy-start | bytes 589828
  185.6 8.8 %collective-permute-start.17 = (bf16[2,96,512]{2,1,0:T(8,128)(2,1)S(1)}, bf16[2,96,512]{2,1,0:T(8,128)(2,1)S(1)}, u32[]{:S(2)}, u32[]{:S(2)}) collective-permute-start(bf16[2,96,512]{2,1,0:T(8,128)(2,1)S(1)} %get-tuple-element.25), channel_id=1, source_target_pairs={{0,24},{4,28},{8,16},{12,20},{16,8},{20,12},{24,0},{28,4},{1,25},{... | collective-permute-start | bytes 589832 | tf_op jit(solution)/shard_map/ppermute | solution.py:338
  187.1 9.8 %collective-permute-start.16 = (bf16[2,96,512]{2,1,0:T(8,128)(2,1)S(1)}, bf16[2,96,512]{2,1,0:T(8,128)(2,1)S(1)}, u32[]{:S(2)}, u32[]{:S(2)}) collective-permute-start(bf16[2,96,512]{2,1,0:T(8,128)(2,1)S(1)} %get-tuple-element.24), channel_id=1, source_target_pairs={{0,16},{4,20},{8,24},{12,28},{16,0},{20,4},{24,8},{28,12},{1,17},{... | collective-permute-start | bytes 589832 | tf_op jit(solution)/shard_map/ppermute | solution.py:338
  188.7 8.3 %collective-permute-start.15 = (bf16[2,96,512]{2,1,0:T(8,128)(2,1)S(1)}, bf16[2,96,512]{2,1,0:T(8,128)(2,1)S(1)}, u32[]{:S(2)}, u32[]{:S(2)}) collective-permute-start(bf16[2,96,512]{2,1,0:T(8,128)(2,1)S(1)} %get-tuple-element.23), channel_id=1, source_target_pairs={{0,8},{4,12},{8,0},{12,4},{16,24},{20,28},{24,16},{28,20},{1,9},{5... | collective-permute-start | bytes 589832 | tf_op jit(solution)/shard_map/ppermute | solution.py:338
  194.5 4.4 %copy-start.19 = (bf16[2,96,512]{2,1,0:T(8,128)(2,1)}, bf16[2,96,512]{2,1,0:T(8,128)(2,1)S(1)}, u32[]{:S(2)}) copy-start(bf16[2,96,512]{2,1,0:T(8,128)(2,1)S(1)} %collective-permute-done.17.refs_3_) | copy-start | bytes 589828
  197.1 1.8 collective-permute-start.18
  201.9 20.0 %collective-permute-start.19 = (bf16[768,512]{1,0:T(8,128)(2,1)}, bf16[768,512]{1,0:T(8,128)(2,1)S(1)}, u32[]{:S(2)}, u32[]{:S(2)}) collective-permute-start(bf16[768,512]{1,0:T(8,128)(2,1)} %bitcast.62), channel_id=1, source_target_pairs={{0,1},{1,2},{2,3},{4,5},{5,6},{6,7},{8,9},{9,10},{10,11},{12,13},{... | collective-permute-start | bytes 2359304 | tf_op jit(solution)/shard_map/ppermute | solution.py:139
  204.6 22.6 %collective-permute-start.21 = (bf16[768,512]{1,0:T(8,128)(2,1)}, bf16[768,512]{1,0:T(8,128)(2,1)S(1)}, u32[]{:S(2)}, u32[]{:S(2)}) collective-permute-start(bf16[768,512]{1,0:T(8,128)(2,1)} %bitcast.63), channel_id=1, source_target_pairs={{3,2},{2,1},{1,0},{7,6},{6,5},{5,4},{11,10},{10,9},{9,8},{15,14},{... | collective-permute-start | bytes 2359304 | tf_op jit(solution)/shard_map/ppermute | solution.py:139
  221.9 6.6 %copy-start.28 = (bf16[768,512]{1,0:T(8,128)(2,1)}, bf16[768,512]{1,0:T(8,128)(2,1)S(1)}, u32[]{:S(2)}) copy-start(bf16[768,512]{1,0:T(8,128)(2,1)S(1)} %collective-permute-done.19.refs_1_) | copy-start | bytes 2359300
  221.9 6.5 %collective-permute-start.20 = (bf16[768,512]{1,0:T(8,128)(2,1)S(1)}, bf16[768,512]{1,0:T(8,128)(2,1)S(1)}, u32[]{:S(2)}, u32[]{:S(2)}) collective-permute-start(bf16[768,512]{1,0:T(8,128)(2,1)S(1)} %collective-permute-done.19.refs_1_), channel_id=1, source_target_pairs={{1,2},{2,3},{5,6},{6,7},{9,10},{10,11},{13,14},{14,15},{17,18},{18... | collective-permute-start | bytes 2359304 | tf_op jit(solution)/shard_map/ppermute | solution.py:139
  227.2 21.7 %collective-permute-start.22 = (bf16[768,512]{1,0:T(8,128)(2,1)S(1)}, bf16[768,512]{1,0:T(8,128)(2,1)S(1)}, u32[]{:S(2)}, u32[]{:S(2)}) collective-permute-start(bf16[768,512]{1,0:T(8,128)(2,1)S(1)} %collective-permute-done.21.refs_2_.refs_3_), channel_id=1, source_target_pairs={{2,1},{1,0},{6,5},{5,4},{10,9},{9,8},{14,13},{13,12},{18,17},{17,1... | collective-permute-start | bytes 2359304 | tf_op jit(solution)/shard_map/ppermute | solution.py:139
  228.5 25.4 %copy-start.16 = (bf16[768,512]{1,0:T(8,128)(2,1)}, bf16[768,512]{1,0:T(8,128)(2,1)S(1)}, u32[]{:S(2)}) copy-start(bf16[768,512]{1,0:T(8,128)(2,1)S(1)} %collective-permute-done.20.refs_5_) | copy-start | bytes 2359300
  248.9 5.0 %copy-start.17 = (bf16[768,512]{1,0:T(8,128)(2,1)}, bf16[768,512]{1,0:T(8,128)(2,1)S(1)}, u32[]{:S(2)}) copy-start(bf16[768,512]{1,0:T(8,128)(2,1)S(1)} %collective-permute-done.22.refs_4_) | copy-start | bytes 2359300
  249.0 4.9 %copy-start.14 = (bf16[768,512]{1,0:T(8,128)(2,1)}, bf16[768,512]{1,0:T(8,128)(2,1)S(1)}, u32[]{:S(2)}) copy-start(bf16[768,512]{1,0:T(8,128)(2,1)S(1)} %broadcast_select_fusion.1.refs_0_) | copy-start | bytes 2359300
  249.0 20.1 %collective-permute-start.23 = (bf16[768,512]{1,0:T(8,128)(2,1)S(1)}, bf16[768,512]{1,0:T(8,128)(2,1)S(1)}, u32[]{:S(2)}, u32[]{:S(2)}) collective-permute-start(bf16[768,512]{1,0:T(8,128)(2,1)S(1)} %broadcast_select_fusion.1.refs_0_), channel_id=1, source_target_pairs={{2,3},{1,0},{6,7},{5,4},{10,11},{9,8},{14,15},{13,12},{18,19},{17,... | collective-permute-start | bytes 2359304 | tf_op jit(solution)/shard_map/ppermute | solution.py:158
  (11 other events, 14.3 us)
Sparse Core Ops, SparseCore 0:
  185.8 50.9 all-gather.2
